TPU v7x, 32 devices: a whole 2x2x4 slice. The times are simulated.
32 devices in a mesh: dp: 2 (over core), gx: 16 (over z, y, x).
Axes of the slice: x: 2, y: 2, z: 4, core: 2. Of those that a mesh axis runs over, the one named last changes fastest.
Arguments:
- features: bfloat16 [2, 16, 32, 8, 256], P('dp', None, 'gx'), may hold values from -6 to 6
- offsets: int32 [2, 3], P('dp'), may hold values from 0 to 255, as said below
- flip_bits: int32 [2, 3], P('dp'), may hold values from 0 to 1
- weight: bfloat16 [27, 16, 16], replicated, may hold values from -0.3125 to 0.3125
- conv_bias: float32 [16], replicated, may hold values from -3 to 3
- cotangent: bfloat16 [2, 16, 32, 8, 256], P('dp', None, 'gx'), may hold values from -6 to 6
Outputs:
- hidden: bfloat16 [2, 16, 32, 8, 256], P('dp', None, 'gx')
- grad_input: bfloat16 [2, 16, 32, 8, 256], P('dp', None, 'gx')
- grad_weight: float32 [27, 16, 16], replicated
- grad_bias: float32 [16], replicated
Inputs may be any that keep to these rules, and one draw needn't show every extreme that they name: `offsets`: column 0 lies in 0 to 31, column 1 in 0 to 7, column 2 in 0 to 255.
All inputs are finite; a program needn't handle non-finite values.
Results may differ from a plain program's by a relative error of at most 0.0075.
Values may be sent and summed in bfloat16 or wider, within the bound.
A program may use at most 64 MiB of HBM per device.

v0:
```python
import math

import jax
import jax.numpy as jnp
from jax import lax
from jax.sharding import PartitionSpec as P

tap_offsets = [
    (shift_x, shift_y, shift_z)
    for shift_x in range(3)
    for shift_y in range(3)
    for shift_z in range(3)
]


def partner_2(block, axis, bit):
    count = lax.axis_size(axis)
    route = []
    for low in range(count):
        high = low | 1 << bit
        if high != low and high < count:
            route += [(low, high), (high, low)]
    return lax.ppermute(block, axis, route)


def shifted(value, axis, steps):
    count = lax.axis_size(axis)
    pairs = [(source, (source + steps) % count) for source in range(count)]
    return lax.ppermute(value, axis, pairs)


def padded_2(shard, sides, width):
    for axis, dim in sides:
        peers, length = (lax.axis_size(axis), shard.shape[dim])
        up = [(i, (i + 1) % peers) for i in range(peers)]
        down = [(j, i) for i, j in up]
        last = lax.slice_in_dim(shard, length - width, length, axis=dim)
        leading = lax.slice_in_dim(shard, 0, width, axis=dim)
        before = lax.ppermute(last, axis, up)
        after = lax.ppermute(leading, axis, down)
        shard = jnp.concatenate([before, shard, after], axis=dim)
    return shard


def permute_axis(volume, offset, mirror_bit, length, dim_index):
    position = jnp.arange(length, dtype=jnp.int32)
    source = jnp.where(mirror_bit == 1, length - 1 - position, position)
    source = jnp.mod(source - offset, length)
    return jnp.take(volume, source, axis=dim_index)


def augment_local(volume, offset, mirror_bits):
    volume = permute_axis(volume, offset[1], mirror_bits[1], volume.shape[2], 2)
    return permute_axis(volume, offset[2], mirror_bits[2], volume.shape[3], 3)


def gelu_parts(pre_act):
    normal_cdf = 0.5 * (1.0 + lax.erf(pre_act * 0.7071067811865476))
    density = jnp.exp(-0.5 * pre_act * pre_act) * 0.3989422804014327
    return (pre_act * normal_cdf, normal_cdf + pre_act * density)


def cut_planes(stacked, begin_at, length):

    def single(volume, first):
        return lax.dynamic_slice_in_dim(volume, first, length, 1)

    return jax.vmap(single)(stacked, begin_at)


def on_device(features, offsets, flip_bits, weight, conv_bias, cotangent):
    planes = features.shape[2]
    devices_x = lax.axis_size("gx")
    levels = devices_x.bit_length() - 1
    length_x = planes * devices_x
    local = jax.vmap(augment_local)(features, offsets, flip_bits)
    mirror_x = (flip_bits[:, 0] == 1)[:, None, None, None, None]
    mirrored = jnp.where(mirror_x, jnp.flip(local, 2), local)
    for bit_level in range(levels):
        partner = partner_2(mirrored, "gx", bit_level)
        mirrored = jnp.where(mirror_x, partner, mirrored)
    effective = jnp.where(flip_bits[:, 0] == 1, jnp.mod(-offsets[:, 0], length_x), offsets[:, 0])
    coarse_steps = effective // planes
    remain = effective % planes
    coarse = mirrored
    for bit_level in range(levels):
        arrived = shifted(coarse, "gx", 2**bit_level)
        taken = (coarse_steps // 2**bit_level % 2 == 1)[:, None, None, None, None]
        coarse = jnp.where(taken, arrived, coarse)
    previous = shifted(coarse, "gx", 1)
    joined = jnp.concatenate([previous, coarse], axis=2)
    augmented = cut_planes(joined, planes - remain, planes)
    padded = padded_2(augmented, (("gx", 2),), 1)
    total = jnp.zeros(features.shape, jnp.float32) + conv_bias[None, :, None, None, None]
    for tap_index, (shift_x, shift_y, shift_z) in enumerate(tap_offsets):
        window = jnp.roll(
            padded[:, :, shift_x : shift_x + planes], (1 - shift_y, 1 - shift_z), axis=(3, 4)
        )
        total = total + jnp.einsum(
            "oi,bixyz->boxyz", weight[tap_index], window, preferred_element_type=jnp.float32
        )
    hidden, slope = gelu_parts(total)
    grad_pre = (cotangent.astype(jnp.float32) * slope).astype(jnp.bfloat16)
    grad_pad = padded_2(grad_pre, (("gx", 2),), 1)
    grad_in = jnp.zeros(features.shape, jnp.float32)
    grad_list = []
    for tap_index, (shift_x, shift_y, shift_z) in enumerate(tap_offsets):
        window = jnp.roll(
            padded[:, :, shift_x : shift_x + planes], (1 - shift_y, 1 - shift_z), axis=(3, 4)
        )
        grad_list.append(
            jnp.einsum("boxyz,bixyz->oi", grad_pre, window, preferred_element_type=jnp.float32)
        )
        moved_grad = jnp.roll(
            grad_pad[:, :, 2 - shift_x : 2 - shift_x + planes],
            (shift_y - 1, shift_z - 1),
            axis=(3, 4),
        )
        grad_in = grad_in + jnp.einsum(
            "oi,boxyz->bixyz", weight[tap_index], moved_grad, preferred_element_type=jnp.float32
        )
    grad_b = jnp.sum(grad_pre.astype(jnp.float32), axis=(0, 2, 3, 4))
    summed_w, summed_b = lax.psum((jnp.stack(grad_list), grad_b), ("dp", "gx"))
    cell_count = (
        features.shape[0] * lax.axis_size("dp") * length_x * features.shape[3] * features.shape[4]
    )
    grad_scale = 1.0 / math.sqrt(cell_count)
    return (
        hidden.astype(jnp.bfloat16),
        grad_in.astype(jnp.bfloat16),
        summed_w * grad_scale,
        summed_b * grad_scale,
    )


def solution(mesh):
    in_specs = (
        P("dp", None, "gx", None, None),
        P("dp", None),
        P("dp", None),
        P(),
        P(),
        P("dp", None, "gx", None, None),
    )
    out_specs = (P("dp", None, "gx", None, None), P("dp", None, "gx", None, None), P(), P())
    return jax.shard_map(
        on_device, mesh=mesh, in_specs=in_specs, out_specs=out_specs, check_vma=False
    )
```

profile of v0, /device:TPU:0, one launch (start us, length us, event | category | flops | bytes accessed | tf_op | source)
XLA Modules:
  0.0 159.4 jit_solution(3923534897879767906)
XLA Ops:
  0.6 1.4 fusion.388
  2.0 1.4 fusion.389
  4.0 0.7 compare_and_fusion.1
  4.7 0.7 compare_select_fusion
  6.0 0.6 compare_select_fusion.4
  6.5 0.6 compare_and_fusion
  7.8 0.9 gather_fusion
  9.4 0.9 gather_fusion.1
  10.4 0.8 copy.70
  11.3 3.0 %collective-permute-start = (bf16[1,16,2,8,256]{4,1,3,2,0:T(8,128)(2,1)S(1)}, bf16[1,16,2,8,256]{4,1,3,2,0:T(8,128)(2,1)S(1)}, u32[]{:S(2)}, u32[]{:S(2)}) collective-permute-start(bf16[1,16,2,8,256]{4,1,3,2,0:T(8,128)(2,1)S(1)} %reverse_select_fusion), channel_id=1, source_target_pairs={{0,1},{1,0},{2,3},{3,2},{4,5},{5,4},{6,7},{7,6},{8,9},{9,8},{10,11... | collective-permute-start | bytes 393224 | tf_op jit(solution)/shard_map/ppermute | solution.py:23
  14.3 3.5 %collective-permute-done = bf16[1,16,2,8,256]{4,1,3,2,0:T(8,128)(2,1)S(1)} collective-permute-done((bf16[1,16,2,8,256]{4,1,3,2,0:T(8,128)(2,1)S(1)}, bf16[1,16,2,8,256]{4,1,3,2,0:T(8,128)(2,1)S(1)}, u32[]{:S(2)}, u32[]{:S(2)}) %collective-permute-start) | collective-permute-done | bytes 131104 | tf_op jit(solution)/shard_map/ppermute | solution.py:23
  17.8 1.8 %collective-permute-start.1 = (bf16[1,16,2,8,256]{4,1,3,2,0:T(8,128)(2,1)S(1)}, bf16[1,16,2,8,256]{4,1,3,2,0:T(8,128)(2,1)S(1)}, u32[]{:S(2)}, u32[]{:S(2)}) collective-permute-start(bf16[1,16,2,8,256]{4,1,3,2,0:T(8,128)(2,1)S(1)} %broadcast_select_fusion.3), channel_id=1, source_target_pairs={{0,2},{2,0},{1,3},{3,1},{4,6},{6,4},{5,7},{7,5},{8,10},{10,8},{9,1... | collective-permute-start | bytes 393224 | tf_op jit(solution)/shard_map/ppermute | solution.py:23
  19.7 3.2 %collective-permute-done.1 = bf16[1,16,2,8,256]{4,1,3,2,0:T(8,128)(2,1)S(1)} collective-permute-done((bf16[1,16,2,8,256]{4,1,3,2,0:T(8,128)(2,1)S(1)}, bf16[1,16,2,8,256]{4,1,3,2,0:T(8,128)(2,1)S(1)}, u32[]{:S(2)}, u32[]{:S(2)}) %collective-permute-start.1) | collective-permute-done | bytes 131104 | tf_op jit(solution)/shard_map/ppermute | solution.py:23
  22.9 1.9 %collective-permute-start.2 = (bf16[1,16,2,8,256]{4,1,3,2,0:T(8,128)(2,1)S(1)}, bf16[1,16,2,8,256]{4,1,3,2,0:T(8,128)(2,1)S(1)}, u32[]{:S(2)}, u32[]{:S(2)}) collective-permute-start(bf16[1,16,2,8,256]{4,1,3,2,0:T(8,128)(2,1)S(1)} %broadcast_select_fusion.2), channel_id=1, source_target_pairs={{0,4},{4,0},{1,5},{5,1},{2,6},{6,2},{3,7},{7,3},{8,12},{12,8},{9,1... | collective-permute-start | bytes 393224 | tf_op jit(solution)/shard_map/ppermute | solution.py:23
  24.8 3.1 %collective-permute-done.2 = bf16[1,16,2,8,256]{4,1,3,2,0:T(8,128)(2,1)S(1)} collective-permute-done((bf16[1,16,2,8,256]{4,1,3,2,0:T(8,128)(2,1)S(1)}, bf16[1,16,2,8,256]{4,1,3,2,0:T(8,128)(2,1)S(1)}, u32[]{:S(2)}, u32[]{:S(2)}) %collective-permute-start.2) | collective-permute-done | bytes 131104 | tf_op jit(solution)/shard_map/ppermute | solution.py:23
  27.9 3.7 %collective-permute-start.3 = (bf16[1,16,2,8,256]{4,1,3,2,0:T(8,128)(2,1)S(1)}, bf16[1,16,2,8,256]{4,1,3,2,0:T(8,128)(2,1)S(1)}, u32[]{:S(2)}, u32[]{:S(2)}) collective-permute-start(bf16[1,16,2,8,256]{4,1,3,2,0:T(8,128)(2,1)S(1)} %broadcast_select_fusion.1), channel_id=1, source_target_pairs={{0,8},{8,0},{1,9},{9,1},{2,10},{10,2},{3,11},{11,3},{4,12},{12,4},... | collective-permute-start | bytes 393224 | tf_op jit(solution)/shard_map/ppermute | solution.py:23
  31.7 4.4 %collective-permute-done.3 = bf16[1,16,2,8,256]{4,1,3,2,0:T(8,128)(2,1)S(1)} collective-permute-done((bf16[1,16,2,8,256]{4,1,3,2,0:T(8,128)(2,1)S(1)}, bf16[1,16,2,8,256]{4,1,3,2,0:T(8,128)(2,1)S(1)}, u32[]{:S(2)}, u32[]{:S(2)}) %collective-permute-start.3) | collective-permute-done | bytes 131104 | tf_op jit(solution)/shard_map/ppermute | solution.py:23
  36.0 1.5 collective-permute-start.4
  39.5 6.4 %collective-permute-done.4 = bf16[1,16,2,8,256]{4,1,3,2,0:T(8,128)(2,1)S(1)} collective-permute-done((bf16[1,16,2,8,256]{4,1,3,2,0:T(8,128)(2,1)S(1)}, bf16[1,16,2,8,256]{4,1,3,2,0:T(8,128)(2,1)S(1)}, u32[]{:S(2)}, u32[]{:S(2)}) %collective-permute-start.4) | collective-permute-done | bytes 131104 | tf_op jit(solution)/shard_map/ppermute | solution.py:29
  46.0 8.0 %collective-permute-done.5 = bf16[1,16,2,8,256]{4,1,3,2,0:T(8,128)(2,1)S(1)} collective-permute-done((bf16[1,16,2,8,256]{4,1,3,2,0:T(8,128)(2,1)S(1)}, bf16[1,16,2,8,256]{4,1,3,2,0:T(8,128)(2,1)S(1)}, u32[]{:S(2)}, u32[]{:S(2)}) %collective-permute-start.5) | collective-permute-done | bytes 131104 | tf_op jit(solution)/shard_map/ppermute | solution.py:29
  54.2 6.7 %collective-permute-done.6 = bf16[1,16,2,8,256]{4,1,3,2,0:T(8,128)(2,1)S(1)} collective-permute-done((bf16[1,16,2,8,256]{4,1,3,2,0:T(8,128)(2,1)S(1)}, bf16[1,16,2,8,256]{4,1,3,2,0:T(8,128)(2,1)S(1)}, u32[]{:S(2)}, u32[]{:S(2)}) %collective-permute-start.6) | collective-permute-done | bytes 131104 | tf_op jit(solution)/shard_map/ppermute | solution.py:29
  62.6 4.2 %collective-permute-done.7 = bf16[1,16,2,8,256]{4,1,3,2,0:T(8,128)(2,1)S(1)} collective-permute-done((bf16[1,16,2,8,256]{4,1,3,2,0:T(8,128)(2,1)S(1)}, bf16[1,16,2,8,256]{4,1,3,2,0:T(8,128)(2,1)S(1)}, u32[]{:S(2)}, u32[]{:S(2)}) %collective-permute-start.7) | collective-permute-done | bytes 131104 | tf_op jit(solution)/shard_map/ppermute | solution.py:29
  70.8 4.7 %collective-permute-done.8 = bf16[1,16,2,8,256]{4,1,3,2,0:T(8,128)(2,1)S(1)} collective-permute-done((bf16[1,16,2,8,256]{4,1,3,2,0:T(8,128)(2,1)S(1)}, bf16[1,16,2,8,256]{4,1,3,2,0:T(8,128)(2,1)S(1)}, u32[]{:S(2)}, u32[]{:S(2)}) %collective-permute-start.8) | collective-permute-done | bytes 131104 | tf_op jit(solution)/shard_map/ppermute | solution.py:29
  75.6 5.6 %collective-permute-start.10 = (bf16[1,16,1,8,256]{4,1,3,2,0:T(8,128)(2,1)S(1)}, bf16[1,16,1,8,256]{4,1,3,2,0:T(8,128)(2,1)S(1)}, u32[]{:S(2)}, u32[]{:S(2)}) collective-permute-start(bf16[1,16,1,8,256]{4,1,3,2,0:T(8,128)(2,1)S(1)} %get-tuple-element.128), channel_id=1, source_target_pairs={{1,0},{2,1},{3,2},{4,3},{5,4},{6,5},{7,6},{8,7},{9,8},{10,9},{11,1... | collective-permute-start | bytes 196616 | tf_op jit(solution)/shard_map/ppermute | solution.py:40
  81.4 2.1 %collective-permute-done.9 = bf16[1,16,1,8,256]{4,1,3,2,0:T(8,128)(2,1)S(1)} collective-permute-done((bf16[1,16,1,8,256]{4,1,3,2,0:T(8,128)(2,1)S(1)}, bf16[1,16,1,8,256]{4,1,3,2,0:T(8,128)(2,1)S(1)}, u32[]{:S(2)}, u32[]{:S(2)}) %collective-permute-start.9) | collective-permute-done | bytes 65568 | tf_op jit(solution)/shard_map/ppermute | solution.py:39
  90.2 0.7 convert_reduce_fusion
  97.1 42.8 %all-reduce = (f32[27,16,16]{2,1,0:T(8,128)S(1)}, f32[16]{0:T(128)S(1)}) all-reduce(f32[27,16,16]{2,1,0:T(8,128)S(1)} %fusion.42, f32[16]{0:T(128)S(1)} %get-tuple-element.25), channel_id=1, replica_groups=mesh['dp'=2,'gx'=16] {'dp','gx'}, use_global_device_ids=true, to_apply=%region_0.1 | all-reduce | flops 6928 | bytes 55424 | tf_op jit(solution)/shard_map/psum | solution.py:123
  139.9 2.5 %collective-permute-start.11 = (bf16[1,16,1,8,256]{4,1,3,2,0:T(8,128)(2,1)S(1)}, bf16[1,16,1,8,256]{4,1,3,2,0:T(8,128)(2,1)S(1)}, u32[]{:S(2)}, u32[]{:S(2)}) collective-permute-start(bf16[1,16,1,8,256]{4,1,3,2,0:T(8,128)(2,1)S(1)} %get-tuple-element.95), channel_id=1, source_target_pairs={{1,0},{2,1},{3,2},{4,3},{5,4},{6,5},{7,6},{8,7},{9,8},{10,9},{11,1... | collective-permute-start | bytes 196616 | tf_op jit(solution)/shard_map/ppermute | solution.py:40
  142.9 0.8 copy.128
  143.7 0.7 copy.126
  144.4 5.8 %collective-permute-done.12 = bf16[1,16,1,8,256]{4,1,3,2,0:T(8,128)(2,1)S(1)} collective-permute-done((bf16[1,16,1,8,256]{4,1,3,2,0:T(8,128)(2,1)S(1)}, bf16[1,16,1,8,256]{4,1,3,2,0:T(8,128)(2,1)S(1)}, u32[]{:S(2)}, u32[]{:S(2)}) %collective-permute-start.12) | collective-permute-done | bytes 65568 | tf_op jit(solution)/shard_map/ppermute | solution.py:39
  158.7 0.7 copy.127
  (174 shorter events, 28.2 us)
Async XLA Ops:
  0.6 7.2 %copy-start = (bf16[1,16,2,8,256]{4,3,2,1,0:T(8,128)(2,1)S(1)}, bf16[1,16,2,8,256]{4,3,2,1,0:T(8,128)(2,1)}, u32[]{:S(2)}) copy-start(bf16[1,16,2,8,256]{4,3,2,1,0:T(8,128)(2,1)} %param.6) | copy-start | bytes 393220
  11.3 6.5 %collective-permute-start = (bf16[1,16,2,8,256]{4,1,3,2,0:T(8,128)(2,1)S(1)}, bf16[1,16,2,8,256]{4,1,3,2,0:T(8,128)(2,1)S(1)}, u32[]{:S(2)}, u32[]{:S(2)}) collective-permute-start(bf16[1,16,2,8,256]{4,1,3,2,0:T(8,128)(2,1)S(1)} %reverse_select_fusion), channel_id=1, source_target_pairs={{0,1},{1,0},{2,3},{3,2},{4,5},{5,4},{6,7},{7,6},{8,9},{9,8},{10,11... | collective-permute-start | bytes 393224 | tf_op jit(solution)/shard_map/ppermute | solution.py:23
  17.8 5.0 %collective-permute-start.1 = (bf16[1,16,2,8,256]{4,1,3,2,0:T(8,128)(2,1)S(1)}, bf16[1,16,2,8,256]{4,1,3,2,0:T(8,128)(2,1)S(1)}, u32[]{:S(2)}, u32[]{:S(2)}) collective-permute-start(bf16[1,16,2,8,256]{4,1,3,2,0:T(8,128)(2,1)S(1)} %broadcast_select_fusion.3), channel_id=1, source_target_pairs={{0,2},{2,0},{1,3},{3,1},{4,6},{6,4},{5,7},{7,5},{8,10},{10,8},{9,1... | collective-permute-start | bytes 393224 | tf_op jit(solution)/shard_map/ppermute | solution.py:23
  22.9 38.1 %copy-start.1 = (bf16[27,16,16]{0,2,1:T(8,128)(2,1)S(1)}, bf16[27,16,16]{0,2,1:T(8,128)(2,1)}, u32[]{:S(2)}) copy-start(bf16[27,16,16]{0,2,1:T(8,128)(2,1)} %param.9) | copy-start | bytes 41476
  22.9 5.0 %collective-permute-start.2 = (bf16[1,16,2,8,256]{4,1,3,2,0:T(8,128)(2,1)S(1)}, bf16[1,16,2,8,256]{4,1,3,2,0:T(8,128)(2,1)S(1)}, u32[]{:S(2)}, u32[]{:S(2)}) collective-permute-start(bf16[1,16,2,8,256]{4,1,3,2,0:T(8,128)(2,1)S(1)} %broadcast_select_fusion.2), channel_id=1, source_target_pairs={{0,4},{4,0},{1,5},{5,1},{2,6},{6,2},{3,7},{7,3},{8,12},{12,8},{9,1... | collective-permute-start | bytes 393224 | tf_op jit(solution)/shard_map/ppermute | solution.py:23
  27.9 8.1 %collective-permute-start.3 = (bf16[1,16,2,8,256]{4,1,3,2,0:T(8,128)(2,1)S(1)}, bf16[1,16,2,8,256]{4,1,3,2,0:T(8,128)(2,1)S(1)}, u32[]{:S(2)}, u32[]{:S(2)}) collective-permute-start(bf16[1,16,2,8,256]{4,1,3,2,0:T(8,128)(2,1)S(1)} %broadcast_select_fusion.1), channel_id=1, source_target_pairs={{0,8},{8,0},{1,9},{9,1},{2,10},{10,2},{3,11},{11,3},{4,12},{12,4},... | collective-permute-start | bytes 393224 | tf_op jit(solution)/shard_map/ppermute | solution.py:23
  36.0 9.9 %collective-permute-start.4 = (bf16[1,16,2,8,256]{4,1,3,2,0:T(8,128)(2,1)S(1)}, bf16[1,16,2,8,256]{4,1,3,2,0:T(8,128)(2,1)S(1)}, u32[]{:S(2)}, u32[]{:S(2)}) collective-permute-start(bf16[1,16,2,8,256]{4,1,3,2,0:T(8,128)(2,1)S(1)} %broadcast_select_fusion), channel_id=1, source_target_pairs={{0,1},{1,2},{2,3},{3,4},{4,5},{5,6},{6,7},{7,8},{8,9},{9,10},{10,1... | collective-permute-start | bytes 393224 | tf_op jit(solution)/shard_map/ppermute | solution.py:29
  45.9 8.1 %collective-permute-start.5 = (bf16[1,16,2,8,256]{4,1,3,2,0:T(8,128)(2,1)S(1)}, bf16[1,16,2,8,256]{4,1,3,2,0:T(8,128)(2,1)S(1)}, u32[]{:S(2)}, u32[]{:S(2)}) collective-permute-start(bf16[1,16,2,8,256]{4,1,3,2,0:T(8,128)(2,1)S(1)} %broadcast_select_fusion.4), channel_id=1, source_target_pairs={{0,2},{1,3},{2,4},{3,5},{4,6},{5,7},{6,8},{7,9},{8,10},{9,11},{10,... | collective-permute-start | bytes 393224 | tf_op jit(solution)/shard_map/ppermute | solution.py:29
  54.1 6.8 %collective-permute-start.6 = (bf16[1,16,2,8,256]{4,1,3,2,0:T(8,128)(2,1)S(1)}, bf16[1,16,2,8,256]{4,1,3,2,0:T(8,128)(2,1)S(1)}, u32[]{:S(2)}, u32[]{:S(2)}) collective-permute-start(bf16[1,16,2,8,256]{4,1,3,2,0:T(8,128)(2,1)S(1)} %broadcast_select_fusion.5), channel_id=1, source_target_pairs={{0,4},{1,5},{2,6},{3,7},{4,8},{5,9},{6,10},{7,11},{8,12},{9,13},{1... | collective-permute-start | bytes 393224 | tf_op jit(solution)/shard_map/ppermute | solution.py:29
  60.9 5.9 %collective-permute-start.7 = (bf16[1,16,2,8,256]{4,1,3,2,0:T(8,128)(2,1)S(1)}, bf16[1,16,2,8,256]{4,1,3,2,0:T(8,128)(2,1)S(1)}, u32[]{:S(2)}, u32[]{:S(2)}) collective-permute-start(bf16[1,16,2,8,256]{4,1,3,2,0:T(8,128)(2,1)S(1)} %broadcast_select_fusion.6), channel_id=1, source_target_pairs={{0,8},{1,9},{2,10},{3,11},{4,12},{5,13},{6,14},{7,15},{8,0},{9,1},... | collective-permute-start | bytes 393224 | tf_op jit(solution)/shard_map/ppermute | solution.py:29
  66.8 8.6 %collective-permute-start.8 = (bf16[1,16,2,8,256]{4,1,3,2,0:T(8,128)(2,1)S(1)}, bf16[1,16,2,8,256]{4,1,3,2,0:T(8,128)(2,1)S(1)}, u32[]{:S(2)}, u32[]{:S(2)}) collective-permute-start(bf16[1,16,2,8,256]{4,1,3,2,0:T(8,128)(2,1)S(1)} %broadcast_select_fusion.7), channel_id=1, source_target_pairs={{0,1},{1,2},{2,3},{3,4},{4,5},{5,6},{6,7},{7,8},{8,9},{9,10},{10,1... | collective-permute-start | bytes 393224 | tf_op jit(solution)/shard_map/ppermute | solution.py:29
  75.6 7.9 %collective-permute-start.9 = (bf16[1,16,1,8,256]{4,1,3,2,0:T(8,128)(2,1)S(1)}, bf16[1,16,1,8,256]{4,1,3,2,0:T(8,128)(2,1)S(1)}, u32[]{:S(2)}, u32[]{:S(2)}) collective-permute-start(bf16[1,16,1,8,256]{4,1,3,2,0:T(8,128)(2,1)S(1)} %get-tuple-element.127), channel_id=1, source_target_pairs={{0,1},{1,2},{2,3},{3,4},{4,5},{5,6},{6,7},{7,8},{8,9},{9,10},{10,1... | collective-permute-start | bytes 196616 | tf_op jit(solution)/shard_map/ppermute | solution.py:39
  75.6 7.9 %collective-permute-start.10 = (bf16[1,16,1,8,256]{4,1,3,2,0:T(8,128)(2,1)S(1)}, bf16[1,16,1,8,256]{4,1,3,2,0:T(8,128)(2,1)S(1)}, u32[]{:S(2)}, u32[]{:S(2)}) collective-permute-start(bf16[1,16,1,8,256]{4,1,3,2,0:T(8,128)(2,1)S(1)} %get-tuple-element.128), channel_id=1, source_target_pairs={{1,0},{2,1},{3,2},{4,3},{5,4},{6,5},{7,6},{8,7},{9,8},{10,9},{11,1... | collective-permute-start | bytes 196616 | tf_op jit(solution)/shard_map/ppermute | solution.py:40
  88.6 1.0 copy-start.3
  89.1 1.1 copy-start.2
  139.9 4.5 %collective-permute-start.11 = (bf16[1,16,1,8,256]{4,1,3,2,0:T(8,128)(2,1)S(1)}, bf16[1,16,1,8,256]{4,1,3,2,0:T(8,128)(2,1)S(1)}, u32[]{:S(2)}, u32[]{:S(2)}) collective-permute-start(bf16[1,16,1,8,256]{4,1,3,2,0:T(8,128)(2,1)S(1)} %get-tuple-element.95), channel_id=1, source_target_pairs={{1,0},{2,1},{3,2},{4,3},{5,4},{6,5},{7,6},{8,7},{9,8},{10,9},{11,1... | collective-permute-start | bytes 196616 | tf_op jit(solution)/shard_map/ppermute | solution.py:40
  142.4 7.9 %collective-permute-start.12 = (bf16[1,16,1,8,256]{4,1,3,2,0:T(8,128)(2,1)S(1)}, bf16[1,16,1,8,256]{4,1,3,2,0:T(8,128)(2,1)S(1)}, u32[]{:S(2)}, u32[]{:S(2)}) collective-permute-start(bf16[1,16,1,8,256]{4,1,3,2,0:T(8,128)(2,1)S(1)} %get-tuple-element.96), channel_id=1, source_target_pairs={{0,1},{1,2},{2,3},{3,4},{4,5},{5,6},{6,7},{7,8},{8,9},{9,10},{10,1... | collective-permute-start | bytes 196616 | tf_op jit(solution)/shard_map/ppermute | solution.py:39
where the time goes:
time: 160 us; the launch traced here: 159 us
  waiting for transfers between devices  52 us (32%)
  blocking collectives  42.8 us (27%)
  starting transfers between devices  20.4 us (13%)
  matrix products  18.9 us (12%)
  local copies, waits for them, and re-layouts  14.6 us (9%)
  between operations  5.52 us (3%)
  other arithmetic  5.15 us (3%)
    psum x1, blocking collectives, on_device(): summed_w, summed_b = lax.psum((jnp.stack(grad_list), grad_b), ('dp', 'gx'))  42.8 us
    ppermute x5, waiting for transfers between devices, shifted(): return lax.ppermute(value, axis, pairs)  29.9 us
    ppermute x4, waiting for transfers between devices, partner_2(): return lax.ppermute(block, axis, route)  14.2 us
    ppermute x4, starting transfers between devices, partner_2(): return lax.ppermute(block, axis, route)  10.5 us
    ppermute x2, starting transfers between devices, padded_2(): after = lax.ppermute(leading, axis, down)  8.1 us
    ppermute x2, waiting for transfers between devices, padded_2(): before = lax.ppermute(last, axis, up)  7.9 us
    unnamed x38, local copies, waits for them, and re-layouts  7.13 us
    dot_general x27, matrix products, on_device(): jnp.einsum('oi,boxyz->bixyz', weight[tap_index], moved_grad, preferred_el...  6.58 us
  transfers between devices with their start and end apart: 13, of which 11 were waited for; matrix products, arithmetic and copies ran while one was open for 5% of the time, Pallas kernels for 0%

commit v1 on v0

v1 whole, which is shorter than its diff:
```python
import functools
import math

import jax
import jax.numpy as jnp
from jax import lax
from jax.experimental import pallas as pl
from jax.experimental.pallas import tpu as pltpu
from jax.sharding import PartitionSpec as P

MESH = pl.DeviceIdType.MESH
bf16, f32 = jnp.bfloat16, jnp.float32


def iota(shape, dim):
    return lax.broadcasted_iota(jnp.int32, shape, dim)


def one_hot(mask):
    return jnp.where(mask, 1.0, 0.0).astype(bf16)


def mm(a, b):
    return jnp.dot(a, b, preferred_element_type=f32)


def mm_t(a, b):
    return lax.dot_general(a, b, (((1,), (1,)), ((), ())), preferred_element_type=f32)


def gelu_parts(pre_act):
    normal_cdf = 0.5 * (1.0 + lax.erf(pre_act * 0.7071067811865476))
    density = jnp.exp(-0.5 * pre_act * pre_act) * 0.3989422804014327
    return (pre_act * normal_cdf, normal_cdf + pre_act * density)


def wait_bytes(ref, sem):
    pltpu.make_async_copy(ref, ref, sem).wait()


def kernel(
    n, dps, planes, ch, ny, nz, scale,
    off_ref, flip_ref, feat_ref, weight_ref, bias_ref, cot_ref,
    hid_ref, gin_ref, gw_ref,
    send1, recv1, stag, recv2, cols, gcols, gext, rs, rsr, dpr, ag,
    send_sems, recv_sems,
):
    me, my_dp = lax.axis_index("gx"), lax.axis_index("dp")
    taps = 27
    rows = ch * planes * ny
    chunks = ny * nz // 128
    nx = n * planes
    per = rs.shape[1]

    barrier = pltpu.get_barrier_semaphore()

    def greet(k, _):
        pl.semaphore_signal(
            barrier, inc=1, device_id={"gx": lax.rem(me + k, n)}, device_id_type=MESH
        )
        return 0

    def greet_dp(k, _):
        pl.semaphore_signal(
            barrier, inc=1, device_id={"dp": lax.rem(my_dp + k, dps)}, device_id_type=MESH
        )
        return 0

    lax.fori_loop(1, n, greet, 0)
    lax.fori_loop(1, dps, greet_dp, 0)

    r_out = iota((rows, rows), 0)
    r_in = iota((rows, rows), 1)
    out_c, out_y, out_x = r_out % ch, (r_out // ch) % ny, r_out // (ch * ny)
    base = (out_c * planes + out_x) * ny
    src_y = jnp.where(flip_ref[0, 1] == 1, ny - 1 - out_y, out_y) - off_ref[0, 1]
    src_y = jnp.bitwise_and(src_y, ny - 1)
    order = one_hot(r_in == base + out_y)
    order_aug = one_hot(r_in == base + src_y)
    zi, zo = iota((nz, nz), 0), iota((nz, nz), 1)
    src_z = jnp.where(flip_ref[0, 2] == 1, nz - 1 - zo, zo) - off_ref[0, 2]
    perm_z = one_hot(zi == jnp.bitwise_and(src_z, nz - 1))
    local = mm(feat_ref[...], perm_z).astype(bf16)
    local = mm(order_aug, local).astype(bf16)
    for j in range(chunks):
        y, half = j // 2, j % 2
        for x in range(planes):
            r0 = (x * ny + y) * ch
            send1[j, x] = local[r0 : r0 + ch, half * 128 : half * 128 + 128]

    pl.semaphore_wait(barrier, n + dps - 2)

    def start1(k, _):
        peer = lax.rem(me + k, n)
        pltpu.make_async_remote_copy(
            src_ref=send1.at[lax.rem(peer, chunks)],
            dst_ref=recv1.at[pl.ds(me * planes, planes)],
            send_sem=send_sems.at[0],
            recv_sem=recv_sems.at[0],
            device_id={"gx": peer},
            device_id_type=MESH,
        ).start()
        return 0

    lax.fori_loop(1, n, start1, 0)
    my_chunk = lax.rem(me, chunks)
    group = me // chunks * chunks
    recv1[pl.ds(me * planes, planes)] = send1[my_chunk]

    width = taps * ch
    w2 = weight_ref[...]
    spread = mm(w2, one_hot(iota((ch, width), 0) == iota((ch, width), 1) % ch))
    same_tap = iota((width, width), 0) // ch == iota((width, width), 1) // ch
    spread = jnp.where(same_tap, spread, 0.0).astype(bf16)
    gather = one_hot(iota((ch, width), 0) == iota((ch, width), 1) % ch)
    w_fwd = mm(gather, spread).astype(bf16)
    eye = one_hot(iota((ch, ch), 0) == iota((ch, ch), 1))
    w_bwd = mm_t(eye, w2).astype(bf16)
    cot = mm(order, cot_ref[...])
    bias = bias_ref[...]
    z_less = one_hot(zi == jnp.bitwise_and(zo - 1, nz - 1))
    z_more = one_hot(zi == jnp.bitwise_and(zo + 1, nz - 1))
    cols[width : width + ch] = jnp.ones((ch, cols.shape[1]), bf16)

    wait_bytes(recv1.at[pl.ds(0, (n - 1) * planes)], recv_sems.at[0])

    for p in range(chunks * planes + 2):
        target = lax.rem(group * planes + (p - 1 + nx), nx)
        source = jnp.where(flip_ref[0, 0] == 1, nx - 1 - target, target) - off_ref[0, 0]
        stag[p] = recv1[lax.rem(source + nx, nx)]

    def start2(k, _):
        q = lax.rem(my_chunk + k, chunks)
        pltpu.make_async_remote_copy(
            src_ref=stag.at[pl.ds(q * planes, planes + 2)],
            dst_ref=recv2.at[my_chunk],
            send_sem=send_sems.at[1],
            recv_sem=recv_sems.at[1],
            device_id={"gx": group + q},
            device_id_type=MESH,
        ).start()
        return 0

    lax.fori_loop(1, chunks, start2, 0)
    recv2[my_chunk] = stag[pl.ds(my_chunk * planes, planes + 2)]
    wait_bytes(recv2.at[pl.ds(0, chunks - 1)], recv_sems.at[1])

    def lane(x, y):
        return (x * ny + y) * nz

    for p in range(planes + 2):
        mid = [
            jnp.concatenate([recv2[2 * y, p], recv2[2 * y + 1, p]], axis=1) for y in range(ny)
        ]
        stacked = jnp.concatenate(mid, axis=0)
        shifts = [mm(stacked, z_less).astype(bf16), stacked, mm(stacked, z_more).astype(bf16)]
        for a in range(3):
            x = p - a
            if not 0 <= x < planes:
                continue
            for e in range(3):
                for h in range(3):
                    t = 9 * a + 3 * e + h
                    for y in range(ny):
                        s = (y + e - 1) % ny
                        cols[t * ch : t * ch + ch, lane(x, y) : lane(x, y) + nz] = shifts[h][
                            s * ch : s * ch + ch
                        ]

    hidden = []
    for x in range(planes):
        for y in range(ny):
            r0 = (x * ny + y) * ch
            at = slice(lane(x, y), lane(x, y) + nz)
            pre = mm(w_fwd, cols[0:width, at]) + bias
            act, slope = gelu_parts(pre)
            hidden.append(act.astype(bf16))
            gext[x + 1, y] = (cot[r0 : r0 + ch] * slope).astype(bf16)

    right, left = lax.rem(me + 1, n), lax.rem(me + n - 1, n)
    halos = [
        pltpu.make_async_remote_copy(
            src_ref=gext.at[here],
            dst_ref=gext.at[there],
            send_sem=send_sems.at[2 + side],
            recv_sem=recv_sems.at[2 + side],
            device_id={"gx": peer},
            device_id_type=MESH,
        )
        for side, (here, there, peer) in enumerate(
            [(planes, 0, right), (1, planes + 1, left)]
        )
    ]
    for halo in halos:
        halo.start()

    gw = jnp.zeros((ch, width + ch), f32)
    for x in range(planes):
        for y in range(ny):
            gw = gw + mm_t(gext[x + 1, y], cols[:, lane(x, y) : lane(x, y) + nz])
    gw = jnp.concatenate([gw, jnp.zeros((ch, 512 - width - ch), f32)], axis=1)
    groups = ch // per
    for k in range(n):
        g, q = k % groups, k // groups
        rs[k] = gw[g * per : g * per + per, q * 128 : q * 128 + 128]

    def start_rs(k, _):
        peer = lax.rem(me + k, n)
        pltpu.make_async_remote_copy(
            src_ref=rs.at[peer],
            dst_ref=rsr.at[me],
            send_sem=send_sems.at[4],
            recv_sem=recv_sems.at[4],
            device_id={"gx": peer},
            device_id_type=MESH,
        ).start()
        return 0

    lax.fori_loop(1, n, start_rs, 0)
    rsr[me] = rs[me]

    hid_ref[...] = lax.dot_general(
        order, jnp.concatenate(hidden, axis=0), (((0,), (0,)), ((), ())),
        preferred_element_type=f32,
    ).astype(bf16)

    def grad_columns(p):
        stacked = jnp.concatenate([gext[p, y] for y in range(ny)], axis=0)
        shifts = [mm(stacked, z_more).astype(bf16), stacked, mm(stacked, z_less).astype(bf16)]
        for a in range(3):
            x = p + a - 2
            if not 0 <= x < planes:
                continue
            for e in range(3):
                for h in range(3):
                    t = 9 * a + 3 * e + h
                    for y in range(ny):
                        s = (y + 1 - e) % ny
                        gcols[t * ch : t * ch + ch, lane(x, y) : lane(x, y) + nz] = shifts[h][
                            s * ch : s * ch + ch
                        ]

    for p in range(1, planes + 1):
        grad_columns(p)

    wait_bytes(rsr.at[pl.ds(0, n - 1)], recv_sems.at[4])
    total = rsr[0]
    for k in range(1, n):
        total = total + rsr[k]
    dpr[my_dp] = total

    def start_dp(k, _):
        pltpu.make_async_remote_copy(
            src_ref=dpr.at[my_dp],
            dst_ref=dpr.at[my_dp],
            send_sem=send_sems.at[5],
            recv_sem=recv_sems.at[5],
            device_id={"dp": lax.rem(my_dp + k, dps)},
            device_id_type=MESH,
        ).start()
        return 0

    lax.fori_loop(1, dps, start_dp, 0)

    for halo in halos:
        halo.wait()
    grad_columns(0)
    grad_columns(planes + 1)

    wait_bytes(dpr.at[pl.ds(0, dps - 1)], recv_sems.at[5])
    total = dpr[0]
    for k in range(1, dps):
        total = total + dpr[k]
    ag[me] = total * scale

    def start_ag(k, _):
        pltpu.make_async_remote_copy(
            src_ref=ag.at[me],
            dst_ref=ag.at[me],
            send_sem=send_sems.at[6],
            recv_sem=recv_sems.at[6],
            device_id={"gx": lax.rem(me + k, n)},
            device_id_type=MESH,
        ).start()
        return 0

    lax.fori_loop(1, n, start_ag, 0)

    grad_in = [
        mm(w_bwd, gcols[:, lane(x, y) : lane(x, y) + nz]).astype(bf16)
        for x in range(planes)
        for y in range(ny)
    ]
    gin_ref[...] = lax.dot_general(
        order, jnp.concatenate(grad_in, axis=0), (((0,), (0,)), ((), ())),
        preferred_element_type=f32,
    ).astype(bf16)

    wait_bytes(ag.at[pl.ds(0, n - 1)], recv_sems.at[6])
    for k in range(n):
        g, q = k % groups, k // groups
        gw_ref[g * per : g * per + per, q * 128 : q * 128 + 128] = ag[k]

    wait_bytes(recv1.at[pl.ds(0, (n - 1) * planes)], send_sems.at[0])
    wait_bytes(recv2.at[pl.ds(0, chunks - 1)], send_sems.at[1])
    wait_bytes(rsr.at[pl.ds(0, n - 1)], send_sems.at[4])
    wait_bytes(dpr.at[pl.ds(0, dps - 1)], send_sems.at[5])
    wait_bytes(ag.at[pl.ds(0, n - 1)], send_sems.at[6])


def on_device(features, offsets, flip_bits, weight, conv_bias, cotangent):
    _, ch, planes, ny, nz = features.shape
    n, dps = lax.axis_size("gx"), lax.axis_size("dp")
    taps = weight.shape[0]
    rows, cells, chunks = ch * planes * ny, planes * ny * nz, ny * nz // 128
    width = taps * ch
    per = ch * 512 // (128 * n)
    scale = 1.0 / math.sqrt(dps * n * cells)
    vmem = pl.BlockSpec(memory_space=pltpu.VMEM)
    smem = pl.BlockSpec(memory_space=pltpu.SMEM)
    hidden, grad_in, grad_w = pl.pallas_call(
        functools.partial(kernel, n, dps, planes, ch, ny, nz, scale),
        out_shape=(
            jax.ShapeDtypeStruct((rows, nz), bf16),
            jax.ShapeDtypeStruct((rows, nz), bf16),
            jax.ShapeDtypeStruct((ch, 512), f32),
        ),
        in_specs=[smem, smem, vmem, vmem, vmem, vmem],
        out_specs=(vmem, vmem, vmem),
        scratch_shapes=[
            pltpu.VMEM((chunks, planes, ch, 128), bf16),
            pltpu.VMEM((n * planes, ch, 128), bf16),
            pltpu.VMEM((chunks * planes + 2, ch, 128), bf16),
            pltpu.VMEM((chunks, planes + 2, ch, 128), bf16),
            pltpu.VMEM((width + ch, cells), bf16),
            pltpu.VMEM((width, cells), bf16),
            pltpu.VMEM((planes + 2, ny, ch, nz), bf16),
            pltpu.VMEM((n, per, 128), f32),
            pltpu.VMEM((n, per, 128), f32),
            pltpu.VMEM((dps, per, 128), f32),
            pltpu.VMEM((n, per, 128), f32),
            pltpu.SemaphoreType.DMA((7,)),
            pltpu.SemaphoreType.DMA((7,)),
        ],
        compiler_params=pltpu.CompilerParams(
            collective_id=0, has_side_effects=True, vmem_limit_bytes=40 * 2**20
        ),
        cost_estimate=pl.CostEstimate(
            flops=6 * ch * width * cells, bytes_accessed=8 * rows * nz, transcendentals=2 * ch * cells
        ),
    )(
        offsets,
        flip_bits,
        features.reshape(rows, nz),
        weight.reshape(width, ch),
        conv_bias.reshape(ch, 1),
        cotangent.reshape(rows, nz),
    )
    grad_weight = grad_w[:, :width].reshape(ch, taps, ch).transpose(1, 0, 2)
    return (
        hidden.reshape(features.shape),
        grad_in.reshape(features.shape),
        grad_weight,
        grad_w[:, width],
    )


def solution(mesh):
    in_specs = (
        P("dp", None, "gx", None, None),
        P("dp", None),
        P("dp", None),
        P(),
        P(),
        P("dp", None, "gx", None, None),
    )
    out_specs = (P("dp", None, "gx", None, None), P("dp", None, "gx", None, None), P(), P())
    return jax.shard_map(
        on_device, mesh=mesh, in_specs=in_specs, out_specs=out_specs, check_vma=False
    )
```

time: 160 us -> 37.2 us (0.23)
  waiting for transfers between devices: 52 us -> 0 us
  blocking collectives: 42.8 us -> 0 us
  Pallas kernels: 0 us -> 30.1 us
  starting transfers between devices: 20.4 us -> 0 us
  matrix products: 18.9 us -> 0 us
  local copies, waits for them, and re-layouts: 14.6 us -> 6.3 us
  other arithmetic: 5.15 us -> 0 us
  between operations: 5.52 us -> 0.68 us
    ppermute x13 -> x0, waiting for transfers between devices: 52 us -> none  [the longest x5 29.9 us: shifted(): return lax.ppermute(value, axis, pairs)]
    psum x1 -> x0, blocking collectives: 42.8 us -> none  [on_device(): summed_w, summed_b = lax.psum((jnp.stack(grad_list), grad_b), ('dp', 'gx'))]
    pallas_call x0 -> x1, Pallas kernels: none -> 30.1 us  [on_device(): pl.pallas_call(functools.partial(kernel, n, dps, planes, ch, ny, nz, scal...]
    ppermute x13 -> x0, starting transfers between devices: 20.4 us -> none  [the longest x4 10.5 us: partner_2(): return lax.ppermute(block, axis, route)]
    dot_general x81 -> x0, matrix products: 18.9 us -> none  [the longest x27 6.58 us: on_device(): jnp.einsum('oi,boxyz->bixyz', weight[tap_index], moved_grad, preferred_el...]
    slice x15 -> x1, local copies, waits for them, and re-layouts: 4.22 us -> 0.69 us  [on_device(): grad_w[:, width]]
    gather x5 -> x0, local copies, waits for them, and re-layouts: 2.74 us -> none  [permute_axis(): return jnp.take(volume, source, axis=dim_index)]
    unnamed x38 -> x12, local copies, waits for them, and re-layouts: 7.13 us -> 4.71 us
  transfers between devices with their start and end apart: 13 -> 0, of which waited for: 11 -> 0; matrix products, arithmetic and copies ran while one was open for 5% -> 0% of each run, Pallas kernels for 0% -> 0%
where the time goes in v1:
time: 37.2 us; the launch traced here: 37 us
  Pallas kernels  30.1 us (81%)
  local copies, waits for them, and re-layouts  6.3 us (17%)
  between operations  0.68 us (2%)
    pallas_call x1, Pallas kernels, on_device(): pl.pallas_call(functools.partial(kernel, n, dps, planes, ch, ny, nz, scal...  30.1 us
    unnamed x12, local copies, waits for them, and re-layouts  4.71 us
    reshape x1, local copies, waits for them, and re-layouts, on_device(): conv_bias.reshape(ch, 1)  0.77 us

profile of v1, /device:TPU:0, one launch (start us, length us, event | category | flops | bytes accessed | tf_op | source)
XLA Modules:
  0.0 37.0 jit_solution(15039716822153526520)
XLA Ops:
  0.6 0.0 copy-start
  0.6 0.8 %copy.14.bias_ref = f32[16,1]{1,0:T(8,128)S(1)} copy(f32[16,1]{0,1:T(1,128)} %bitcast.15) | data formatting | bytes 128 | tf_op jit(solution)/shard_map/reshape | solution.py:356
  1.4 1.0 %copy.13 = bf16[27,16,16]{2,1,0:T(8,128)(2,1)S(1)} copy(bf16[27,16,16]{0,2,1:T(8,128)(2,1)} %param.9) | data formatting | bytes 27648 | tf_op args[3]
  2.4 0.0 copy-start.2
  2.4 0.0 copy-start.3
  2.5 0.0 copy-done
  2.5 0.6 %copy-done.2 = s32[1,3]{1,0:T(1,128)S(1)} copy-done((s32[1,3]{1,0:T(1,128)S(1)}, s32[1,3]{1,0:T(1,128)}, u32[]{:S(2)}) %copy-start.2) | copy-done | bytes 36
  3.1 0.0 copy-done.3
  3.1 0.0 copy-start.1
  3.1 0.9 %copy-done.1 = bf16[1,16,2,8,256]{4,3,2,1,0:T(8,128)(2,1)S(1)} copy-done((bf16[1,16,2,8,256]{4,3,2,1,0:T(8,128)(2,1)S(1)}, bf16[1,16,2,8,256]{4,3,2,1,0:T(8,128)(2,1)}, u32[]{:S(2)}) %copy-start.1) | copy-done | bytes 131096
  4.0 30.1 %shard_map.93 = (bf16[256,256]{1,0:T(8,128)(2,1)S(1)}, bf16[256,256]{1,0:T(8,128)(2,1)S(1)}, f32[16,512]{1,0:T(8,128)S(1)}) custom-call(s32[1,3]{1,0:T(1,128)S(1)} %copy-done.2, s32[1,3]{1,0:T(1,128)S(1)} %copy-done.3, bf16[256,256]{1,0:T(8,128)(2,1)S(1)} %bitcast.12, bf16[432,16]{1,0:T(8,128)(2,1)S(1)} %bitcast.10, f32[16,1]{1,0:T(8,128)S(1)} %copy.14.bias_ref, ...), custom_call_target="tpu_custom_call" | custom-call | flops 169869312 | bytes 524288 | tf_op jit(solution)/shard_map/pallas_call | solution.py:321
  34.1 0.7 %slice_reduce_fusion = f32[16]{0:T(128)} fusion(f32[16,512]{1,0:T(8,128)S(1)} %get-tuple-element.9), kind=kLoop, calls=%fused_computation | loop fusion | bytes 128 | tf_op jit(solution)/shard_map/slice | solution.py:364
  34.8 0.1 reshape.35
  34.9 0.8 %copy.15 = f32[27,16,16]{0,2,1:T(8,128)} copy(f32[27,16,16]{2,0,1:T(8,128)S(1)} %bitcast.14) | data formatting | bytes 55296
  35.7 0.7 %copy.18 = bf16[1,16,2,8,256]{4,3,2,1,0:T(8,128)(2,1)} copy(bf16[1,16,2,8,256]{4,3,2,1,0:T(8,128)(2,1)S(1)} %bitcast.9) | data formatting | bytes 262144
  36.4 0.7 %copy.19 = bf16[1,16,2,8,256]{4,3,2,1,0:T(8,128)(2,1)} copy(bf16[1,16,2,8,256]{4,3,2,1,0:T(8,128)(2,1)S(1)} %bitcast.8) | data formatting | bytes 262144
Async XLA Ops:
  0.6 1.8 %copy-start = (bf16[1,16,2,8,256]{4,3,2,1,0:T(8,128)(2,1)S(1)}, bf16[1,16,2,8,256]{4,3,2,1,0:T(8,128)(2,1)}, u32[]{:S(2)}) copy-start(bf16[1,16,2,8,256]{4,3,2,1,0:T(8,128)(2,1)} %param.6) | copy-start | bytes 393220
  2.4 0.7 %copy-start.2 = (s32[1,3]{1,0:T(1,128)S(1)}, s32[1,3]{1,0:T(1,128)}, u32[]{:S(2)}) copy-start(s32[1,3]{1,0:T(1,128)} %off_ref.1) | copy-start | bytes 40
  2.4 0.7 %copy-start.3 = (s32[1,3]{1,0:T(1,128)S(1)}, s32[1,3]{1,0:T(1,128)}, u32[]{:S(2)}) copy-start(s32[1,3]{1,0:T(1,128)} %flip_ref.1) | copy-start | bytes 40
  3.1 0.9 %copy-start.1 = (bf16[1,16,2,8,256]{4,3,2,1,0:T(8,128)(2,1)S(1)}, bf16[1,16,2,8,256]{4,3,2,1,0:T(8,128)(2,1)}, u32[]{:S(2)}) copy-start(bf16[1,16,2,8,256]{4,3,2,1,0:T(8,128)(2,1)} %param.11) | copy-start | bytes 393220

commit v2 on v1

--- a/solution.py
+++ b/solution.py
@@ -41,9 +41,9 @@
 def kernel(
     n, dps, planes, ch, ny, nz, scale,
     off_ref, flip_ref, feat_ref, weight_ref, bias_ref, cot_ref,
-    hid_ref, gin_ref, gw_ref,
-    send1, recv1, stag, recv2, cols, gcols, gext, rs, rsr, dpr, ag,
-    send_sems, recv_sems,
+    hid_out, gin_out, gw_out,
+    hid_ref, gin_ref, gw_ref, feat, weight, cot_in, send1, recv1, stag, recv2, cols, gcols, gext, rs, rsr, dpr, ag,
+    load_sems, store_sems, send_sems, recv_sems,
 ):
     me, my_dp = lax.axis_index("gx"), lax.axis_index("dp")
     taps = 27
@@ -52,6 +52,21 @@
     nx = n * planes
     per = rs.shape[1]
 
+    loads = [
+        pltpu.make_async_copy(source, target, load_sems.at[k])
+        for k, (source, target) in enumerate(
+            [(feat_ref, feat), (weight_ref, weight), (cot_ref, cot_in)]
+        )
+    ]
+    for load in loads:
+        load.start()
+    stores = [
+        pltpu.make_async_copy(source, target, store_sems.at[k])
+        for k, (source, target) in enumerate(
+            [(hid_ref, hid_out), (gin_ref, gin_out), (gw_ref, gw_out)]
+        )
+    ]
+
     barrier = pltpu.get_barrier_semaphore()
 
     def greet(k, _):
@@ -69,18 +84,18 @@
     lax.fori_loop(1, n, greet, 0)
     lax.fori_loop(1, dps, greet_dp, 0)
 
-    r_out = iota((rows, rows), 0)
-    r_in = iota((rows, rows), 1)
-    out_c, out_y, out_x = r_out % ch, (r_out // ch) % ny, r_out // (ch * ny)
+    r_out = iota((rows, 1), 0)
+    r_in = iota((1, rows), 1)
+    out_c, out_y, out_x = r_out & (ch - 1), (r_out // ch) & (ny - 1), r_out // (ch * ny)
     base = (out_c * planes + out_x) * ny
     src_y = jnp.where(flip_ref[0, 1] == 1, ny - 1 - out_y, out_y) - off_ref[0, 1]
-    src_y = jnp.bitwise_and(src_y, ny - 1)
     order = one_hot(r_in == base + out_y)
-    order_aug = one_hot(r_in == base + src_y)
-    zi, zo = iota((nz, nz), 0), iota((nz, nz), 1)
+    order_aug = one_hot(r_in == base + (src_y & (ny - 1)))
+    zi, zo = iota((nz, 1), 0), iota((1, nz), 1)
     src_z = jnp.where(flip_ref[0, 2] == 1, nz - 1 - zo, zo) - off_ref[0, 2]
-    perm_z = one_hot(zi == jnp.bitwise_and(src_z, nz - 1))
-    local = mm(feat_ref[...], perm_z).astype(bf16)
+    perm_z = one_hot(zi == (src_z & (nz - 1)))
+    loads[0].wait()
+    local = mm(feat[...], perm_z).astype(bf16)
     local = mm(order_aug, local).astype(bf16)
     for j in range(chunks):
         y, half = j // 2, j % 2
@@ -108,49 +123,67 @@
     recv1[pl.ds(me * planes, planes)] = send1[my_chunk]
 
     width = taps * ch
-    w2 = weight_ref[...]
-    spread = mm(w2, one_hot(iota((ch, width), 0) == iota((ch, width), 1) % ch))
-    same_tap = iota((width, width), 0) // ch == iota((width, width), 1) // ch
-    spread = jnp.where(same_tap, spread, 0.0).astype(bf16)
-    gather = one_hot(iota((ch, width), 0) == iota((ch, width), 1) % ch)
-    w_fwd = mm(gather, spread).astype(bf16)
-    eye = one_hot(iota((ch, ch), 0) == iota((ch, ch), 1))
-    w_bwd = mm_t(eye, w2).astype(bf16)
-    cot = mm(order, cot_ref[...])
-    bias = bias_ref[...]
-    z_less = one_hot(zi == jnp.bitwise_and(zo - 1, nz - 1))
-    z_more = one_hot(zi == jnp.bitwise_and(zo + 1, nz - 1))
+    loads[1].wait()
+    tap_of = one_hot(iota((taps, 1), 0) == iota((1, width), 1) // ch)
+    spread = mm(weight[...], tap_of)
+    pair, lane_c = iota((ch * ch, 1), 0), iota((1, width), 1) & (ch - 1)
+    by_in = jnp.where((pair & (ch - 1)) == lane_c, spread, 0.0).astype(bf16)
+    by_out = jnp.where(pair // ch == lane_c, spread, 0.0).astype(bf16)
+    row, across = iota((ch, 1), 0), iota((1, ch * ch), 1)
+    w_fwd = mm(one_hot(row == across // ch), by_in).astype(bf16)
+    w_bwd = mm(one_hot(row == (across & (ch - 1))), by_out).astype(bf16)
+    bias = jnp.sum(
+        jnp.where(iota((ch, 1), 0) == iota((1, ch), 1), bias_ref[...], 0.0), axis=1, keepdims=True
+    )
+    z_less = one_hot(zi == ((zo - 1) & (nz - 1)))
+    z_more = one_hot(zi == ((zo + 1) & (nz - 1)))
     cols[width : width + ch] = jnp.ones((ch, cols.shape[1]), bf16)
+    loads[2].wait()
+    cot = mm(order, cot_in[...])
 
     wait_bytes(recv1.at[pl.ds(0, (n - 1) * planes)], recv_sems.at[0])
 
-    for p in range(chunks * planes + 2):
+    def routed(p):
         target = lax.rem(group * planes + (p - 1 + nx), nx)
         source = jnp.where(flip_ref[0, 0] == 1, nx - 1 - target, target) - off_ref[0, 0]
-        stag[p] = recv1[lax.rem(source + nx, nx)]
-
-    def start2(k, _):
+        return recv1[lax.rem(source + nx, nx)]
+
+    first, last = planes, planes + 1
+    for q in range(chunks):
+        for x in range(planes):
+            plane = routed(q * planes + x + 1)
+            stag[q, x] = plane
+            if x == planes - 1:
+                stag[(q + 1) % chunks, first] = plane
+            if x == 0:
+                stag[(q - 1) % chunks, last] = plane
+    stag[0, first] = routed(0)
+    stag[chunks - 1, last] = routed(chunks * planes + 1)
+
+    def start2(begin, count, k, _):
         q = lax.rem(my_chunk + k, chunks)
         pltpu.make_async_remote_copy(
-            src_ref=stag.at[pl.ds(q * planes, planes + 2)],
-            dst_ref=recv2.at[my_chunk],
-            send_sem=send_sems.at[1],
-            recv_sem=recv_sems.at[1],
+            src_ref=stag.at[q, pl.ds(begin, count)],
+            dst_ref=recv2.at[my_chunk, pl.ds(begin, count)],
+            send_sem=send_sems.at[1 if begin == 0 else 7],
+            recv_sem=recv_sems.at[1 if begin == 0 else 7],
             device_id={"gx": group + q},
             device_id_type=MESH,
         ).start()
         return 0
 
-    lax.fori_loop(1, chunks, start2, 0)
-    recv2[my_chunk] = stag[pl.ds(my_chunk * planes, planes + 2)]
-    wait_bytes(recv2.at[pl.ds(0, chunks - 1)], recv_sems.at[1])
+    lax.fori_loop(1, chunks, functools.partial(start2, 0, planes), 0)
+    lax.fori_loop(1, chunks, functools.partial(start2, planes, 2), 0)
+    recv2[my_chunk] = stag[my_chunk]
 
     def lane(x, y):
         return (x * ny + y) * nz
 
-    for p in range(planes + 2):
+    def columns(p):
+        slot = first if p == 0 else last if p == planes + 1 else p - 1
         mid = [
-            jnp.concatenate([recv2[2 * y, p], recv2[2 * y + 1, p]], axis=1) for y in range(ny)
+            jnp.concatenate([recv2[2 * y, slot], recv2[2 * y + 1, slot]], axis=1)
+            for y in range(ny)
         ]
         stacked = jnp.concatenate(mid, axis=0)
         shifts = [mm(stacked, z_less).astype(bf16), stacked, mm(stacked, z_more).astype(bf16)]
@@ -167,14 +200,20 @@
                             s * ch : s * ch + ch
                         ]
 
-    hidden = []
+    wait_bytes(recv2.at[pl.ds(0, chunks - 1), pl.ds(0, planes)], recv_sems.at[1])
+    for p in range(1, planes + 1):
+        columns(p)
+    wait_bytes(recv2.at[pl.ds(0, chunks - 1), pl.ds(planes, 2)], recv_sems.at[7])
+    columns(0)
+    columns(planes + 1)
+
     for x in range(planes):
         for y in range(ny):
             r0 = (x * ny + y) * ch
             at = slice(lane(x, y), lane(x, y) + nz)
             pre = mm(w_fwd, cols[0:width, at]) + bias
             act, slope = gelu_parts(pre)
-            hidden.append(act.astype(bf16))
+            hid_ref[r0 : r0 + ch] = act.astype(bf16)
             gext[x + 1, y] = (cot[r0 : r0 + ch] * slope).astype(bf16)
 
     right, left = lax.rem(me + 1, n), lax.rem(me + n - 1, n)
@@ -218,11 +257,7 @@
 
     lax.fori_loop(1, n, start_rs, 0)
     rsr[me] = rs[me]
-
-    hid_ref[...] = lax.dot_general(
-        order, jnp.concatenate(hidden, axis=0), (((0,), (0,)), ((), ())),
-        preferred_element_type=f32,
-    ).astype(bf16)
+    stores[0].start()
 
     def grad_columns(p):
         stacked = jnp.concatenate([gext[p, y] for y in range(ny)], axis=0)
@@ -286,26 +321,78 @@
 
     lax.fori_loop(1, n, start_ag, 0)
 
-    grad_in = [
-        mm(w_bwd, gcols[:, lane(x, y) : lane(x, y) + nz]).astype(bf16)
-        for x in range(planes)
-        for y in range(ny)
-    ]
-    gin_ref[...] = lax.dot_general(
-        order, jnp.concatenate(grad_in, axis=0), (((0,), (0,)), ((), ())),
-        preferred_element_type=f32,
-    ).astype(bf16)
-
+    for x in range(planes):
+        for y in range(ny):
+            r0 = (x * ny + y) * ch
+            grad = mm(w_bwd, gcols[:, lane(x, y) : lane(x, y) + nz])
+            gin_ref[r0 : r0 + ch] = grad.astype(bf16)
+
+    stores[1].start()
     wait_bytes(ag.at[pl.ds(0, n - 1)], recv_sems.at[6])
     for k in range(n):
         g, q = k % groups, k // groups
         gw_ref[g * per : g * per + per, q * 128 : q * 128 + 128] = ag[k]
 
+    stores[2].start()
     wait_bytes(recv1.at[pl.ds(0, (n - 1) * planes)], send_sems.at[0])
-    wait_bytes(recv2.at[pl.ds(0, chunks - 1)], send_sems.at[1])
+    wait_bytes(recv2.at[pl.ds(0, chunks - 1), pl.ds(0, planes)], send_sems.at[1])
+    wait_bytes(recv2.at[pl.ds(0, chunks - 1), pl.ds(planes, 2)], send_sems.at[7])
     wait_bytes(rsr.at[pl.ds(0, n - 1)], send_sems.at[4])
     wait_bytes(dpr.at[pl.ds(0, dps - 1)], send_sems.at[5])
     wait_bytes(ag.at[pl.ds(0, n - 1)], send_sems.at[6])
+    for store in stores:
+        store.wait()
+
+
+def finish(
+    planes, ch, ny, nz, taps,
+    hid_in, gin_in, gw_in,
+    hid_out, gin_out, gw_out, gb_out,
+    hid_ref, gin_ref, gw_ref, hid, gin, gw, gb, load_sems, sems,
+):
+    rows, width = ch * planes * ny, taps * ch
+    loads = [
+        pltpu.make_async_copy(source, target, load_sems.at[k])
+        for k, (source, target) in enumerate(
+            [(hid_in, hid_ref), (gin_in, gin_ref), (gw_in, gw_ref)]
+        )
+    ]
+    for load in loads:
+        load.start()
+    stores = [
+        pltpu.make_async_copy(source, target, sems.at[k])
+        for k, (source, target) in enumerate(
+            [(hid, hid_out), (gin, gin_out), (gw, gw_out), (gb, gb_out)]
+        )
+    ]
+    r_in, r_out = iota((rows, 1), 0), iota((1, rows), 1)
+    base = ((r_out & (ch - 1)) * planes + r_out // (ch * ny)) * ny
+    order = one_hot(r_in == base + ((r_out // ch) & (ny - 1)))
+    loads[0].wait()
+    hid[...] = mm(order, hid_ref[...]).astype(bf16)
+    stores[0].start()
+    loads[1].wait()
+    gin[...] = mm(order, gin_ref[...]).astype(bf16)
+    stores[1].start()
+    loads[2].wait()
+    kept = (iota((ch, 1), 0)) == (iota((1, width), 1) & (ch - 1))
+    pairs = jnp.concatenate(
+        [jnp.where(kept, gw_ref[o : o + 1, 0:width], 0.0) for o in range(ch)], axis=0
+    )
+    tap_of = one_hot(iota((width, 1), 0) // ch == iota((1, taps), 1))
+    high = pairs.astype(bf16)
+    rest = pairs - high.astype(f32)
+    mid = rest.astype(bf16)
+    low = (rest - mid.astype(f32)).astype(bf16)
+    gw[...] = mm(high, tap_of) + (mm(mid, tap_of) + mm(low, tap_of))
+    stores[2].start()
+    gb[...] = jnp.sum(
+        jnp.where(iota((ch, 1), 0) == iota((1, ch), 1), gw_ref[:, width : width + 1], 0.0),
+        axis=0, keepdims=True,
+    )
+    stores[3].start()
+    for store in stores:
+        store.wait()
 
 
 def on_device(features, offsets, flip_bits, weight, conv_bias, cotangent):
@@ -318,6 +405,7 @@
     scale = 1.0 / math.sqrt(dps * n * cells)
     vmem = pl.BlockSpec(memory_space=pltpu.VMEM)
     smem = pl.BlockSpec(memory_space=pltpu.SMEM)
+    hbm = pl.BlockSpec(memory_space=pltpu.HBM)
     hidden, grad_in, grad_w = pl.pallas_call(
         functools.partial(kernel, n, dps, planes, ch, ny, nz, scale),
         out_shape=(
@@ -325,12 +413,18 @@
             jax.ShapeDtypeStruct((rows, nz), bf16),
             jax.ShapeDtypeStruct((ch, 512), f32),
         ),
-        in_specs=[smem, smem, vmem, vmem, vmem, vmem],
-        out_specs=(vmem, vmem, vmem),
+        in_specs=[smem, smem, hbm, hbm, vmem, hbm],
+        out_specs=(hbm, hbm, hbm),
         scratch_shapes=[
+            pltpu.VMEM((rows, nz), bf16),
+            pltpu.VMEM((rows, nz), bf16),
+            pltpu.VMEM((ch, 512), f32),
+            pltpu.VMEM((rows, nz), bf16),
+            pltpu.VMEM((ch * ch, taps), bf16),
+            pltpu.VMEM((rows, nz), bf16),
             pltpu.VMEM((chunks, planes, ch, 128), bf16),
             pltpu.VMEM((n * planes, ch, 128), bf16),
-            pltpu.VMEM((chunks * planes + 2, ch, 128), bf16),
+            pltpu.VMEM((chunks, planes + 2, ch, 128), bf16),
             pltpu.VMEM((chunks, planes + 2, ch, 128), bf16),
             pltpu.VMEM((width + ch, cells), bf16),
             pltpu.VMEM((width, cells), bf16),
@@ -339,11 +433,13 @@
             pltpu.VMEM((n, per, 128), f32),
             pltpu.VMEM((dps, per, 128), f32),
             pltpu.VMEM((n, per, 128), f32),
-            pltpu.SemaphoreType.DMA((7,)),
-            pltpu.SemaphoreType.DMA((7,)),
+            pltpu.SemaphoreType.DMA((3,)),
+            pltpu.SemaphoreType.DMA((3,)),
+            pltpu.SemaphoreType.DMA((8,)),
+            pltpu.SemaphoreType.DMA((8,)),
         ],
         compiler_params=pltpu.CompilerParams(
-            collective_id=0, has_side_effects=True, vmem_limit_bytes=40 * 2**20
+            collective_id=0, has_side_effects=True, vmem_limit_bytes=63 * 2**20
         ),
         cost_estimate=pl.CostEstimate(
             flops=6 * ch * width * cells, bytes_accessed=8 * rows * nz, transcendentals=2 * ch * cells
@@ -352,16 +448,38 @@
         offsets,
         flip_bits,
         features.reshape(rows, nz),
-        weight.reshape(width, ch),
-        conv_bias.reshape(ch, 1),
+        weight.transpose(1, 2, 0).reshape(ch * ch, taps),
+        conv_bias.reshape(1, ch),
         cotangent.reshape(rows, nz),
     )
-    grad_weight = grad_w[:, :width].reshape(ch, taps, ch).transpose(1, 0, 2)
+    hidden, grad_in, grad_w, grad_b = pl.pallas_call(
+        functools.partial(finish, planes, ch, ny, nz, taps),
+        out_shape=(
+            jax.ShapeDtypeStruct((rows, nz), bf16),
+            jax.ShapeDtypeStruct((rows, nz), bf16),
+            jax.ShapeDtypeStruct((ch * ch, taps), f32),
+            jax.ShapeDtypeStruct((1, ch), f32),
+        ),
+        in_specs=[hbm, hbm, hbm],
+        out_specs=(hbm, hbm, hbm, hbm),
+        scratch_shapes=[
+            pltpu.VMEM((rows, nz), bf16),
+            pltpu.VMEM((rows, nz), bf16),
+            pltpu.VMEM((ch, 512), f32),
+            pltpu.VMEM((rows, nz), bf16),
+            pltpu.VMEM((rows, nz), bf16),
+            pltpu.VMEM((ch * ch, taps), f32),
+            pltpu.VMEM((1, ch), f32),
+            pltpu.SemaphoreType.DMA((3,)),
+            pltpu.SemaphoreType.DMA((4,)),
+        ],
+        compiler_params=pltpu.CompilerParams(vmem_limit_bytes=63 * 2**20),
+    )(hidden, grad_in, grad_w)
     return (
         hidden.reshape(features.shape),
         grad_in.reshape(features.shape),
-        grad_weight,
-        grad_w[:, width],
+        grad_w.reshape(ch, ch, taps).transpose(2, 0, 1),
+        grad_b.reshape(ch),
     )
 
 

time: 37.2 us -> 34.5 us (0.927)
  local copies, waits for them, and re-layouts: 6.3 us -> 0 us
  Pallas kernels: 30.1 us -> 33.7 us
    unnamed x12 -> x0, local copies, waits for them, and re-layouts: 4.71 us -> none
    pallas_call x0 -> x1, Pallas kernels: none -> 2.47 us  [on_device(): pl.pallas_call(functools.partial(finish, planes, ch, ny, nz, taps), out_s...]
    pallas_call x1, Pallas kernels: 30.1 us -> 31.3 us  [on_device(): pl.pallas_call(functools.partial(kernel, n, dps, planes, ch, ny, nz, scal...]
    reshape x2 -> x0, local copies, waits for them, and re-layouts: 0.9 us -> none  [the longest x1 0.77 us: on_device(): conv_bias.reshape(ch, 1)]
    slice x1 -> x0, local copies, waits for them, and re-layouts: 0.69 us -> none  [on_device(): grad_w[:, width]]
where the time goes in v2:
time: 34.5 us; the launch traced here: 34.4 us
  Pallas kernels  33.7 us (98%)
  between operations  0.64 us (2%)
    pallas_call x1, Pallas kernels, on_device(): pl.pallas_call(functools.partial(kernel, n, dps, planes, ch, ny, nz, scal...  31.3 us
    pallas_call x1, Pallas kernels, on_device(): pl.pallas_call(functools.partial(finish, planes, ch, ny, nz, taps), out_s...  2.47 us

profile of v2, /device:TPU:0, one launch (start us, length us, event | category | flops | bytes accessed | tf_op | source)
XLA Modules:
  0.0 34.4 jit_solution(12685254446306116951)
XLA Ops:
  0.6 31.3 %shard_map.93 = (bf16[256,256]{1,0:T(8,128)(2,1)}, bf16[256,256]{1,0:T(8,128)(2,1)}, f32[16,512]{1,0:T(8,128)}) custom-call(s32[1,3]{1,0:T(1,128)} %off_ref.1, s32[1,3]{1,0:T(1,128)} %flip_ref.1, bf16[256,256]{1,0:T(8,128)(2,1)} %bitcast.12, bf16[256,27]{1,0:T(8,128)(2,1)} %bitcast.17, f32[1,16]{1,0:T(1,128)} %bitcast.18, bf16[256,256]{1,0:T(8,128)(2,1)} %bitcast.13), custom_call_target="tpu_custom_call" | custom-call | flops 169869312 | bytes 524288 | tf_op jit(solution)/shard_map/pallas_call | solution.py:409
  31.9 2.5 %shard_map.94 = (bf16[256,256]{1,0:T(8,128)(2,1)}, bf16[256,256]{1,0:T(8,128)(2,1)}, f32[256,27]{1,0:T(8,128)}, f32[1,16]{1,0:T(1,128)}) custom-call(bf16[256,256]{1,0:T(8,128)(2,1)} %get-tuple-element.11.hid_in, bf16[256,256]{1,0:T(8,128)(2,1)} %get-tuple-element.12.gin_in, f32[16,512]{1,0:T(8,128)} %get-tuple-element.13.gw_in), custom_call_target="tpu_custom_call" | custom-call | tf_op jit(solution)/shard_map/pallas_call | solution.py:455

commit v3 on v2

--- a/solution.py
+++ b/solution.py
@@ -32,6 +32,16 @@
     normal_cdf = 0.5 * (1.0 + lax.erf(pre_act * 0.7071067811865476))
     density = jnp.exp(-0.5 * pre_act * pre_act) * 0.3989422804014327
     return (pre_act * normal_cdf, normal_cdf + pre_act * density)
+
+
+def wrap(index, count):
+    if count & (count - 1) == 0:
+        return index & (count - 1)
+    return lax.rem(index + count, count)
+
+
+def each_peer(count, body):
+    lax.fori_loop(1, count, lambda k, _: body(k) or 0, 0, unroll=count <= 16)
 
 
 def wait_bytes(ref, sem):
@@ -69,20 +79,18 @@
 
     barrier = pltpu.get_barrier_semaphore()
 
-    def greet(k, _):
+    def greet(k):
         pl.semaphore_signal(
-            barrier, inc=1, device_id={"gx": lax.rem(me + k, n)}, device_id_type=MESH
-        )
-        return 0
-
-    def greet_dp(k, _):
+            barrier, inc=1, device_id={"gx": wrap(me + k, n)}, device_id_type=MESH
+        )
+
+    def greet_dp(k):
         pl.semaphore_signal(
-            barrier, inc=1, device_id={"dp": lax.rem(my_dp + k, dps)}, device_id_type=MESH
-        )
-        return 0
-
-    lax.fori_loop(1, n, greet, 0)
-    lax.fori_loop(1, dps, greet_dp, 0)
+            barrier, inc=1, device_id={"dp": wrap(my_dp + k, dps)}, device_id_type=MESH
+        )
+
+    each_peer(n, greet)
+    each_peer(dps, greet_dp)
 
     r_out = iota((rows, 1), 0)
     r_in = iota((1, rows), 1)
@@ -105,20 +113,19 @@
 
     pl.semaphore_wait(barrier, n + dps - 2)
 
-    def start1(k, _):
-        peer = lax.rem(me + k, n)
-        pltpu.make_async_remote_copy(
-            src_ref=send1.at[lax.rem(peer, chunks)],
+    def start1(k):
+        peer = wrap(me + k, n)
+        pltpu.make_async_remote_copy(
+            src_ref=send1.at[wrap(peer, chunks)],
             dst_ref=recv1.at[pl.ds(me * planes, planes)],
             send_sem=send_sems.at[0],
             recv_sem=recv_sems.at[0],
             device_id={"gx": peer},
             device_id_type=MESH,
         ).start()
-        return 0
-
-    lax.fori_loop(1, n, start1, 0)
-    my_chunk = lax.rem(me, chunks)
+
+    each_peer(n, start1)
+    my_chunk = wrap(me, chunks)
     group = me // chunks * chunks
     recv1[pl.ds(me * planes, planes)] = send1[my_chunk]
 
@@ -141,12 +148,16 @@
     loads[2].wait()
     cot = mm(order, cot_in[...])
 
+    sources = []
+    for p in range(chunks * planes + 2):
+        target = wrap(group * planes + (p - 1), nx)
+        source = jnp.where(flip_ref[0, 0] == 1, nx - 1 - target, target) - off_ref[0, 0]
+        sources.append(wrap(source, nx))
+
     wait_bytes(recv1.at[pl.ds(0, (n - 1) * planes)], recv_sems.at[0])
 
     def routed(p):
-        target = lax.rem(group * planes + (p - 1 + nx), nx)
-        source = jnp.where(flip_ref[0, 0] == 1, nx - 1 - target, target) - off_ref[0, 0]
-        return recv1[lax.rem(source + nx, nx)]
+        return recv1[sources[p]]
 
     first, last = planes, planes + 1
     for q in range(chunks):
@@ -160,8 +171,8 @@
     stag[0, first] = routed(0)
     stag[chunks - 1, last] = routed(chunks * planes + 1)
 
-    def start2(begin, count, k, _):
-        q = lax.rem(my_chunk + k, chunks)
+    def start2(begin, count, k):
+        q = wrap(my_chunk + k, chunks)
         pltpu.make_async_remote_copy(
             src_ref=stag.at[q, pl.ds(begin, count)],
             dst_ref=recv2.at[my_chunk, pl.ds(begin, count)],
@@ -170,10 +181,9 @@
             device_id={"gx": group + q},
             device_id_type=MESH,
         ).start()
-        return 0
-
-    lax.fori_loop(1, chunks, functools.partial(start2, 0, planes), 0)
-    lax.fori_loop(1, chunks, functools.partial(start2, planes, 2), 0)
+
+    each_peer(chunks, functools.partial(start2, 0, planes))
+    each_peer(chunks, functools.partial(start2, planes, 2))
     recv2[my_chunk] = stag[my_chunk]
 
     def lane(x, y):
@@ -207,14 +217,18 @@
     columns(0)
     columns(planes + 1)
 
+    hidden, gw = [], jnp.zeros((width + ch, ch), f32)
     for x in range(planes):
+        grads = []
         for y in range(ny):
             r0 = (x * ny + y) * ch
             at = slice(lane(x, y), lane(x, y) + nz)
             pre = mm(w_fwd, cols[0:width, at]) + bias
             act, slope = gelu_parts(pre)
-            hid_ref[r0 : r0 + ch] = act.astype(bf16)
-            gext[x + 1, y] = (cot[r0 : r0 + ch] * slope).astype(bf16)
+            hidden.append(act.astype(bf16))
+            grads.append((cot[r0 : r0 + ch] * slope).astype(bf16))
+            gext[x + 1, y] = grads[-1]
+        gw = gw + mm_t(cols[:, lane(x, 0) : lane(x, 0) + ny * nz], jnp.concatenate(grads, axis=1))
 
     right, left = lax.rem(me + 1, n), lax.rem(me + n - 1, n)
     halos = [
@@ -233,18 +247,14 @@
     for halo in halos:
         halo.start()
 
-    gw = jnp.zeros((ch, width + ch), f32)
-    for x in range(planes):
-        for y in range(ny):
-            gw = gw + mm_t(gext[x + 1, y], cols[:, lane(x, y) : lane(x, y) + nz])
-    gw = jnp.concatenate([gw, jnp.zeros((ch, 512 - width - ch), f32)], axis=1)
+    gw = jnp.concatenate([gw, jnp.zeros((512 - width - ch, ch), f32)], axis=0).T
     groups = ch // per
     for k in range(n):
         g, q = k % groups, k // groups
         rs[k] = gw[g * per : g * per + per, q * 128 : q * 128 + 128]
 
-    def start_rs(k, _):
-        peer = lax.rem(me + k, n)
+    def start_rs(k):
+        peer = wrap(me + k, n)
         pltpu.make_async_remote_copy(
             src_ref=rs.at[peer],
             dst_ref=rsr.at[me],
@@ -253,10 +263,14 @@
             device_id={"gx": peer},
             device_id_type=MESH,
         ).start()
-        return 0
-
-    lax.fori_loop(1, n, start_rs, 0)
+
+    each_peer(n, start_rs)
     rsr[me] = rs[me]
+
+    b_out, b_in = iota((rows, 1), 0), iota((1, rows), 1)
+    b_base = ((b_in & (ch - 1)) * planes + b_in // (ch * ny)) * ny
+    back = one_hot(b_out == b_base + ((b_in // ch) & (ny - 1)))
+    hid_ref[...] = mm(back, jnp.concatenate(hidden, axis=0)).astype(bf16)
     stores[0].start()
 
     def grad_columns(p):
@@ -284,18 +298,17 @@
         total = total + rsr[k]
     dpr[my_dp] = total
 
-    def start_dp(k, _):
+    def start_dp(k):
         pltpu.make_async_remote_copy(
             src_ref=dpr.at[my_dp],
             dst_ref=dpr.at[my_dp],
             send_sem=send_sems.at[5],
             recv_sem=recv_sems.at[5],
-            device_id={"dp": lax.rem(my_dp + k, dps)},
+            device_id={"dp": wrap(my_dp + k, dps)},
             device_id_type=MESH,
         ).start()
-        return 0
-
-    lax.fori_loop(1, dps, start_dp, 0)
+
+    each_peer(dps, start_dp)
 
     for halo in halos:
         halo.wait()
@@ -308,24 +321,24 @@
         total = total + dpr[k]
     ag[me] = total * scale
 
-    def start_ag(k, _):
+    def start_ag(k):
         pltpu.make_async_remote_copy(
             src_ref=ag.at[me],
             dst_ref=ag.at[me],
             send_sem=send_sems.at[6],
             recv_sem=recv_sems.at[6],
-            device_id={"gx": lax.rem(me + k, n)},
+            device_id={"gx": wrap(me + k, n)},
             device_id_type=MESH,
         ).start()
-        return 0
-
-    lax.fori_loop(1, n, start_ag, 0)
-
-    for x in range(planes):
-        for y in range(ny):
-            r0 = (x * ny + y) * ch
-            grad = mm(w_bwd, gcols[:, lane(x, y) : lane(x, y) + nz])
-            gin_ref[r0 : r0 + ch] = grad.astype(bf16)
+
+    each_peer(n, start_ag)
+
+    grad_in = [
+        mm(w_bwd, gcols[:, lane(x, y) : lane(x, y) + nz]).astype(bf16)
+        for x in range(planes)
+        for y in range(ny)
+    ]
+    gin_ref[...] = mm(back, jnp.concatenate(grad_in, axis=0)).astype(bf16)
 
     stores[1].start()
     wait_bytes(ag.at[pl.ds(0, n - 1)], recv_sems.at[6])
@@ -345,41 +358,25 @@
 
 
 def finish(
-    planes, ch, ny, nz, taps,
-    hid_in, gin_in, gw_in,
-    hid_out, gin_out, gw_out, gb_out,
-    hid_ref, gin_ref, gw_ref, hid, gin, gw, gb, load_sems, sems,
+    ch, taps, hid_in, gin_in, gw_in, hid_out, gin_out, gw_out, gb_out, gw_ref, gw, gb, load_sem, sems
 ):
-    rows, width = ch * planes * ny, taps * ch
-    loads = [
-        pltpu.make_async_copy(source, target, load_sems.at[k])
-        for k, (source, target) in enumerate(
-            [(hid_in, hid_ref), (gin_in, gin_ref), (gw_in, gw_ref)]
-        )
-    ]
-    for load in loads:
-        load.start()
+    width = taps * ch
+    load = pltpu.make_async_copy(gw_in, gw_ref, load_sem)
+    load.start()
     stores = [
         pltpu.make_async_copy(source, target, sems.at[k])
         for k, (source, target) in enumerate(
-            [(hid, hid_out), (gin, gin_out), (gw, gw_out), (gb, gb_out)]
+            [(hid_in, hid_out), (gin_in, gin_out), (gw, gw_out), (gb, gb_out)]
         )
     ]
-    r_in, r_out = iota((rows, 1), 0), iota((1, rows), 1)
-    base = ((r_out & (ch - 1)) * planes + r_out // (ch * ny)) * ny
-    order = one_hot(r_in == base + ((r_out // ch) & (ny - 1)))
-    loads[0].wait()
-    hid[...] = mm(order, hid_ref[...]).astype(bf16)
     stores[0].start()
-    loads[1].wait()
-    gin[...] = mm(order, gin_ref[...]).astype(bf16)
     stores[1].start()
-    loads[2].wait()
-    kept = (iota((ch, 1), 0)) == (iota((1, width), 1) & (ch - 1))
+    kept = iota((ch, 1), 0) == (iota((1, width), 1) & (ch - 1))
+    tap_of = one_hot(iota((width, 1), 0) // ch == iota((1, taps), 1))
+    load.wait()
     pairs = jnp.concatenate(
         [jnp.where(kept, gw_ref[o : o + 1, 0:width], 0.0) for o in range(ch)], axis=0
     )
-    tap_of = one_hot(iota((width, 1), 0) // ch == iota((1, taps), 1))
     high = pairs.astype(bf16)
     rest = pairs - high.astype(f32)
     mid = rest.astype(bf16)
@@ -453,7 +450,7 @@
         cotangent.reshape(rows, nz),
     )
     hidden, grad_in, grad_w, grad_b = pl.pallas_call(
-        functools.partial(finish, planes, ch, ny, nz, taps),
+        functools.partial(finish, ch, taps),
         out_shape=(
             jax.ShapeDtypeStruct((rows, nz), bf16),
             jax.ShapeDtypeStruct((rows, nz), bf16),
@@ -463,14 +460,10 @@
         in_specs=[hbm, hbm, hbm],
         out_specs=(hbm, hbm, hbm, hbm),
         scratch_shapes=[
-            pltpu.VMEM((rows, nz), bf16),
-            pltpu.VMEM((rows, nz), bf16),
             pltpu.VMEM((ch, 512), f32),
-            pltpu.VMEM((rows, nz), bf16),
-            pltpu.VMEM((rows, nz), bf16),
             pltpu.VMEM((ch * ch, taps), f32),
             pltpu.VMEM((1, ch), f32),
-            pltpu.SemaphoreType.DMA((3,)),
+            pltpu.SemaphoreType.DMA,
             pltpu.SemaphoreType.DMA((4,)),
         ],
         compiler_params=pltpu.CompilerParams(vmem_limit_bytes=63 * 2**20),

time: 34.5 us -> 43.1 us (1.25)
  Pallas kernels: 33.7 us -> 42.3 us
    pallas_call x1, Pallas kernels: 2.47 us -> 9.09 us  [on_device(): pl.pallas_call(functools.partial(finish, ch, taps), out_shape=(jax.ShapeD...]
    pallas_call x1, Pallas kernels: 31.3 us -> 33.2 us  [on_device(): pl.pallas_call(functools.partial(kernel, n, dps, planes, ch, ny, nz, scal...]
where the time goes in v3:
time: 43.1 us; the launch traced here: 42.9 us
  Pallas kernels  42.3 us (98%)
  between operations  0.64 us (1%)
    pallas_call x1, Pallas kernels, on_device(): pl.pallas_call(functools.partial(kernel, n, dps, planes, ch, ny, nz, scal...  33.2 us
    pallas_call x1, Pallas kernels, on_device(): pl.pallas_call(functools.partial(finish, ch, taps), out_shape=(jax.ShapeD...  9.09 us

profile of v3, /device:TPU:0, one launch (start us, length us, event | category | flops | bytes accessed | tf_op | source)
XLA Modules:
  0.0 42.9 jit_solution(6931595617785326206)
XLA Ops:
  0.6 33.2 %shard_map.93 = (bf16[256,256]{1,0:T(8,128)(2,1)}, bf16[256,256]{1,0:T(8,128)(2,1)}, f32[16,512]{1,0:T(8,128)}) custom-call(s32[1,3]{1,0:T(1,128)} %off_ref.1, s32[1,3]{1,0:T(1,128)} %flip_ref.1, bf16[256,256]{1,0:T(8,128)(2,1)} %bitcast.12, bf16[256,27]{1,0:T(8,128)(2,1)} %bitcast.17, f32[1,16]{1,0:T(1,128)} %bitcast.18, bf16[256,256]{1,0:T(8,128)(2,1)} %bitcast.13), custom_call_target="tpu_custom_call" | custom-call | flops 169869312 | bytes 524288 | tf_op jit(solution)/shard_map/pallas_call | solution.py:406
  33.8 9.1 %shard_map.94 = (bf16[256,256]{1,0:T(8,128)(2,1)}, bf16[256,256]{1,0:T(8,128)(2,1)}, f32[256,27]{1,0:T(8,128)}, f32[1,16]{1,0:T(1,128)}) custom-call(bf16[256,256]{1,0:T(8,128)(2,1)} %get-tuple-element.11.hid_in, bf16[256,256]{1,0:T(8,128)(2,1)} %get-tuple-element.12.gin_in, f32[16,512]{1,0:T(8,128)} %get-tuple-element.13.gw_in), custom_call_target="tpu_custom_call" | custom-call | tf_op jit(solution)/shard_map/pallas_call | solution.py:452

commit v4 on v3

--- a/solution.py
+++ b/solution.py
@@ -217,18 +217,15 @@
     columns(0)
     columns(planes + 1)
 
-    hidden, gw = [], jnp.zeros((width + ch, ch), f32)
+    hidden = []
     for x in range(planes):
-        grads = []
         for y in range(ny):
             r0 = (x * ny + y) * ch
             at = slice(lane(x, y), lane(x, y) + nz)
             pre = mm(w_fwd, cols[0:width, at]) + bias
             act, slope = gelu_parts(pre)
             hidden.append(act.astype(bf16))
-            grads.append((cot[r0 : r0 + ch] * slope).astype(bf16))
-            gext[x + 1, y] = grads[-1]
-        gw = gw + mm_t(cols[:, lane(x, 0) : lane(x, 0) + ny * nz], jnp.concatenate(grads, axis=1))
+            gext[x + 1, y] = (cot[r0 : r0 + ch] * slope).astype(bf16)
 
     right, left = lax.rem(me + 1, n), lax.rem(me + n - 1, n)
     halos = [
@@ -244,10 +241,11 @@
             [(planes, 0, right), (1, planes + 1, left)]
         )
     ]
-    for halo in halos:
-        halo.start()
-
-    gw = jnp.concatenate([gw, jnp.zeros((512 - width - ch, ch), f32)], axis=0).T
+    gw = jnp.zeros((ch, width + ch), f32)
+    for x in range(planes):
+        for y in range(ny):
+            gw = gw + mm_t(gext[x + 1, y], cols[:, lane(x, y) : lane(x, y) + nz])
+    gw = jnp.concatenate([gw, jnp.zeros((ch, 512 - width - ch), f32)], axis=1)
     groups = ch // per
     for k in range(n):
         g, q = k % groups, k // groups
@@ -266,6 +264,8 @@
 
     each_peer(n, start_rs)
     rsr[me] = rs[me]
+    for halo in halos:
+        halo.start()
 
     b_out, b_in = iota((rows, 1), 0), iota((1, rows), 1)
     b_base = ((b_in & (ch - 1)) * planes + b_in // (ch * ny)) * ny
@@ -358,22 +358,28 @@
 
 
 def finish(
-    ch, taps, hid_in, gin_in, gw_in, hid_out, gin_out, gw_out, gb_out, gw_ref, gw, gb, load_sem, sems
+    ch, taps, hid_in, gin_in, gw_in, hid_out, gin_out, gw_out, gb_out,
+    gw_ref, hid, gin, gw, gb, load_sems, sems,
 ):
     width = taps * ch
-    load = pltpu.make_async_copy(gw_in, gw_ref, load_sem)
-    load.start()
+    loads = [
+        pltpu.make_async_copy(source, target, load_sems.at[k])
+        for k, (source, target) in enumerate([(hid_in, hid), (gin_in, gin), (gw_in, gw_ref)])
+    ]
+    for k in (2, 0, 1):
+        loads[k].start()
     stores = [
         pltpu.make_async_copy(source, target, sems.at[k])
         for k, (source, target) in enumerate(
-            [(hid_in, hid_out), (gin_in, gin_out), (gw, gw_out), (gb, gb_out)]
-        )
-    ]
+            [(hid, hid_out), (gin, gin_out), (gw, gw_out), (gb, gb_out)]
+        )
+    ]
+    kept = iota((ch, 1), 0) == (iota((1, width), 1) & (ch - 1))
+    tap_of = one_hot(iota((width, 1), 0) // ch == iota((1, taps), 1))
+    for k in (2, 0, 1):
+        loads[k].wait()
     stores[0].start()
     stores[1].start()
-    kept = iota((ch, 1), 0) == (iota((1, width), 1) & (ch - 1))
-    tap_of = one_hot(iota((width, 1), 0) // ch == iota((1, taps), 1))
-    load.wait()
     pairs = jnp.concatenate(
         [jnp.where(kept, gw_ref[o : o + 1, 0:width], 0.0) for o in range(ch)], axis=0
     )
@@ -461,9 +467,11 @@
         out_specs=(hbm, hbm, hbm, hbm),
         scratch_shapes=[
             pltpu.VMEM((ch, 512), f32),
+            pltpu.VMEM((rows, nz), bf16),
+            pltpu.VMEM((rows, nz), bf16),
             pltpu.VMEM((ch * ch, taps), f32),
             pltpu.VMEM((1, ch), f32),
-            pltpu.SemaphoreType.DMA,
+            pltpu.SemaphoreType.DMA((3,)),
             pltpu.SemaphoreType.DMA((4,)),
         ],
         compiler_params=pltpu.CompilerParams(vmem_limit_bytes=63 * 2**20),

time: 43.1 us -> 35.2 us (0.82)
  Pallas kernels: 42.3 us -> 34.4 us
    pallas_call x1, Pallas kernels: 9.09 us -> 2.09 us  [on_device(): pl.pallas_call(functools.partial(finish, ch, taps), out_shape=(jax.ShapeD...]
    pallas_call x1, Pallas kernels: 33.2 us -> 32.3 us  [on_device(): pl.pallas_call(functools.partial(kernel, n, dps, planes, ch, ny, nz, scal...]
where the time goes in v4:
time: 35.2 us; the launch traced here: 35 us
  Pallas kernels  34.4 us (98%)
  between operations  0.64 us (2%)
    pallas_call x1, Pallas kernels, on_device(): pl.pallas_call(functools.partial(kernel, n, dps, planes, ch, ny, nz, scal...  32.3 us
    pallas_call x1, Pallas kernels, on_device(): pl.pallas_call(functools.partial(finish, ch, taps), out_shape=(jax.ShapeD...  2.09 us

profile of v4, /device:TPU:0, one launch (start us, length us, event | category | flops | bytes accessed | tf_op | source)
XLA Modules:
  0.0 35.0 jit_solution(13990239633122505373)
XLA Ops:
  0.6 32.3 %shard_map.93 = (bf16[256,256]{1,0:T(8,128)(2,1)}, bf16[256,256]{1,0:T(8,128)(2,1)}, f32[16,512]{1,0:T(8,128)}) custom-call(s32[1,3]{1,0:T(1,128)} %off_ref.1, s32[1,3]{1,0:T(1,128)} %flip_ref.1, bf16[256,256]{1,0:T(8,128)(2,1)} %bitcast.12, bf16[256,27]{1,0:T(8,128)(2,1)} %bitcast.17, f32[1,16]{1,0:T(1,128)} %bitcast.18, bf16[256,256]{1,0:T(8,128)(2,1)} %bitcast.13), custom_call_target="tpu_custom_call" | custom-call | flops 169869312 | bytes 524288 | tf_op jit(solution)/shard_map/pallas_call | solution.py:412
  32.9 2.1 %shard_map.94 = (bf16[256,256]{1,0:T(8,128)(2,1)}, bf16[256,256]{1,0:T(8,128)(2,1)}, f32[256,27]{1,0:T(8,128)}, f32[1,16]{1,0:T(1,128)}) custom-call(bf16[256,256]{1,0:T(8,128)(2,1)} %get-tuple-element.11.hid_in, bf16[256,256]{1,0:T(8,128)(2,1)} %get-tuple-element.12.gin_in, f32[16,512]{1,0:T(8,128)} %get-tuple-element.13.gw_in), custom_call_target="tpu_custom_call" | custom-call | tf_op jit(solution)/shard_map/pallas_call | solution.py:458

commit v5 on v4

--- a/solution.py
+++ b/solution.py
@@ -52,7 +52,7 @@
     n, dps, planes, ch, ny, nz, scale,
     off_ref, flip_ref, feat_ref, weight_ref, bias_ref, cot_ref,
     hid_out, gin_out, gw_out,
-    hid_ref, gin_ref, gw_ref, feat, weight, cot_in, send1, recv1, stag, recv2, cols, gcols, gext, rs, rsr, dpr, ag,
+    hid_ref, gin_ref, gw_ref, feat, weight, cot_in, send1, recv1, stag, recv2, cols, gcols, gext, rs, rsr, zr, ag,
     load_sems, store_sems, send_sems, recv_sems,
 ):
     me, my_dp = lax.axis_index("gx"), lax.axis_index("dp")
@@ -84,13 +84,20 @@
             barrier, inc=1, device_id={"gx": wrap(me + k, n)}, device_id_type=MESH
         )
 
-    def greet_dp(k):
+    layer, heights = 4 * dps, n // 4
+    low, high = me & 3, me // 4
+    mine = my_dp * 4 + low
+
+    def layer_peer(q):
+        return {"dp": q // 4, "gx": high * 4 + (q & 3)}
+
+    def greet_layer(k):
         pl.semaphore_signal(
-            barrier, inc=1, device_id={"dp": wrap(my_dp + k, dps)}, device_id_type=MESH
+            barrier, inc=1, device_id=layer_peer(wrap(my_dp * 4 + 3 + k, layer)), device_id_type=MESH
         )
 
     each_peer(n, greet)
-    each_peer(dps, greet_dp)
+    each_peer(layer - 3, greet_layer)
 
     r_out = iota((rows, 1), 0)
     r_in = iota((1, rows), 1)
@@ -111,7 +118,7 @@
             r0 = (x * ny + y) * ch
             send1[j, x] = local[r0 : r0 + ch, half * 128 : half * 128 + 128]
 
-    pl.semaphore_wait(barrier, n + dps - 2)
+    pl.semaphore_wait(barrier, n - 1 + layer - 4)
 
     def start1(k):
         peer = wrap(me + k, n)
@@ -213,6 +220,14 @@
     wait_bytes(recv2.at[pl.ds(0, chunks - 1), pl.ds(0, planes)], recv_sems.at[1])
     for p in range(1, planes + 1):
         columns(p)
+
+    part = []
+    for x in range(planes):
+        k0, k1 = max(0, 1 - x) * 9 * ch, min(3, planes + 1 - x) * 9 * ch
+        for y in range(ny):
+            at = slice(lane(x, y), lane(x, y) + nz)
+            part.append(mm(w_fwd[:, k0:k1], cols[k0:k1, at]) + bias)
+
     wait_bytes(recv2.at[pl.ds(0, chunks - 1), pl.ds(planes, 2)], recv_sems.at[7])
     columns(0)
     columns(planes + 1)
@@ -222,7 +237,11 @@
         for y in range(ny):
             r0 = (x * ny + y) * ch
             at = slice(lane(x, y), lane(x, y) + nz)
-            pre = mm(w_fwd, cols[0:width, at]) + bias
+            pre = part[x * ny + y]
+            if x == 0:
+                pre = pre + mm(w_fwd[:, : 9 * ch], cols[: 9 * ch, at])
+            if x == planes - 1:
+                pre = pre + mm(w_fwd[:, 18 * ch :], cols[18 * ch : width, at])
             act, slope = gelu_parts(pre)
             hidden.append(act.astype(bf16))
             gext[x + 1, y] = (cot[r0 : r0 + ch] * slope).astype(bf16)
@@ -247,23 +266,23 @@
             gw = gw + mm_t(gext[x + 1, y], cols[:, lane(x, y) : lane(x, y) + nz])
     gw = jnp.concatenate([gw, jnp.zeros((ch, 512 - width - ch), f32)], axis=1)
     groups = ch // per
-    for k in range(n):
+    for k in range(layer):
         g, q = k % groups, k // groups
         rs[k] = gw[g * per : g * per + per, q * 128 : q * 128 + 128]
 
     def start_rs(k):
-        peer = wrap(me + k, n)
+        peer = wrap(mine + k, layer)
         pltpu.make_async_remote_copy(
             src_ref=rs.at[peer],
-            dst_ref=rsr.at[me],
+            dst_ref=rsr.at[mine],
             send_sem=send_sems.at[4],
             recv_sem=recv_sems.at[4],
-            device_id={"gx": peer},
+            device_id=layer_peer(peer),
             device_id_type=MESH,
         ).start()
 
-    each_peer(n, start_rs)
-    rsr[me] = rs[me]
+    each_peer(layer, start_rs)
+    rsr[mine] = rs[mine]
     for halo in halos:
         halo.start()
 
@@ -292,46 +311,46 @@
     for p in range(1, planes + 1):
         grad_columns(p)
 
-    wait_bytes(rsr.at[pl.ds(0, n - 1)], recv_sems.at[4])
+    wait_bytes(rsr.at[pl.ds(0, layer - 1)], recv_sems.at[4])
     total = rsr[0]
-    for k in range(1, n):
+    for k in range(1, layer):
         total = total + rsr[k]
-    dpr[my_dp] = total
-
-    def start_dp(k):
+    zr[high] = total
+
+    def start_z(k):
         pltpu.make_async_remote_copy(
-            src_ref=dpr.at[my_dp],
-            dst_ref=dpr.at[my_dp],
+            src_ref=zr.at[high],
+            dst_ref=zr.at[high],
             send_sem=send_sems.at[5],
             recv_sem=recv_sems.at[5],
-            device_id={"dp": wrap(my_dp + k, dps)},
+            device_id={"gx": wrap(high + k, heights) * 4 + low},
             device_id_type=MESH,
         ).start()
 
-    each_peer(dps, start_dp)
+    each_peer(heights, start_z)
 
     for halo in halos:
         halo.wait()
     grad_columns(0)
     grad_columns(planes + 1)
 
-    wait_bytes(dpr.at[pl.ds(0, dps - 1)], recv_sems.at[5])
-    total = dpr[0]
-    for k in range(1, dps):
-        total = total + dpr[k]
-    ag[me] = total * scale
+    wait_bytes(zr.at[pl.ds(0, heights - 1)], recv_sems.at[5])
+    total = zr[0]
+    for k in range(1, heights):
+        total = total + zr[k]
+    ag[mine] = total * scale
 
     def start_ag(k):
         pltpu.make_async_remote_copy(
-            src_ref=ag.at[me],
-            dst_ref=ag.at[me],
+            src_ref=ag.at[mine],
+            dst_ref=ag.at[mine],
             send_sem=send_sems.at[6],
             recv_sem=recv_sems.at[6],
-            device_id={"gx": wrap(me + k, n)},
+            device_id=layer_peer(wrap(mine + k, layer)),
             device_id_type=MESH,
         ).start()
 
-    each_peer(n, start_ag)
+    each_peer(layer, start_ag)
 
     grad_in = [
         mm(w_bwd, gcols[:, lane(x, y) : lane(x, y) + nz]).astype(bf16)
@@ -341,8 +360,8 @@
     gin_ref[...] = mm(back, jnp.concatenate(grad_in, axis=0)).astype(bf16)
 
     stores[1].start()
-    wait_bytes(ag.at[pl.ds(0, n - 1)], recv_sems.at[6])
-    for k in range(n):
+    wait_bytes(ag.at[pl.ds(0, layer - 1)], recv_sems.at[6])
+    for k in range(layer):
         g, q = k % groups, k // groups
         gw_ref[g * per : g * per + per, q * 128 : q * 128 + 128] = ag[k]
 
@@ -350,9 +369,9 @@
     wait_bytes(recv1.at[pl.ds(0, (n - 1) * planes)], send_sems.at[0])
     wait_bytes(recv2.at[pl.ds(0, chunks - 1), pl.ds(0, planes)], send_sems.at[1])
     wait_bytes(recv2.at[pl.ds(0, chunks - 1), pl.ds(planes, 2)], send_sems.at[7])
-    wait_bytes(rsr.at[pl.ds(0, n - 1)], send_sems.at[4])
-    wait_bytes(dpr.at[pl.ds(0, dps - 1)], send_sems.at[5])
-    wait_bytes(ag.at[pl.ds(0, n - 1)], send_sems.at[6])
+    wait_bytes(rsr.at[pl.ds(0, layer - 1)], send_sems.at[4])
+    wait_bytes(zr.at[pl.ds(0, heights - 1)], send_sems.at[5])
+    wait_bytes(ag.at[pl.ds(0, layer - 1)], send_sems.at[6])
     for store in stores:
         store.wait()
 
@@ -404,7 +423,8 @@
     taps = weight.shape[0]
     rows, cells, chunks = ch * planes * ny, planes * ny * nz, ny * nz // 128
     width = taps * ch
-    per = ch * 512 // (128 * n)
+    layer = 4 * dps
+    per = ch * 512 // (128 * layer)
     scale = 1.0 / math.sqrt(dps * n * cells)
     vmem = pl.BlockSpec(memory_space=pltpu.VMEM)
     smem = pl.BlockSpec(memory_space=pltpu.SMEM)
@@ -432,10 +452,10 @@
             pltpu.VMEM((width + ch, cells), bf16),
             pltpu.VMEM((width, cells), bf16),
             pltpu.VMEM((planes + 2, ny, ch, nz), bf16),
-            pltpu.VMEM((n, per, 128), f32),
-            pltpu.VMEM((n, per, 128), f32),
-            pltpu.VMEM((dps, per, 128), f32),
-            pltpu.VMEM((n, per, 128), f32),
+            pltpu.VMEM((layer, per, 128), f32),
+            pltpu.VMEM((layer, per, 128), f32),
+            pltpu.VMEM((n // 4, per, 128), f32),
+            pltpu.VMEM((layer, per, 128), f32),
             pltpu.SemaphoreType.DMA((3,)),
             pltpu.SemaphoreType.DMA((3,)),
             pltpu.SemaphoreType.DMA((8,)),

time: 35.2 us -> 34.7 us (0.986)
  Pallas kernels: 34.4 us -> 33.9 us
    pallas_call x1, Pallas kernels: 32.3 us -> 31.8 us  [on_device(): pl.pallas_call(functools.partial(kernel, n, dps, planes, ch, ny, nz, scal...]
where the time goes in v5:
time: 34.7 us; the launch traced here: 34.5 us
  Pallas kernels  33.9 us (98%)
  between operations  0.64 us (2%)
    pallas_call x1, Pallas kernels, on_device(): pl.pallas_call(functools.partial(kernel, n, dps, planes, ch, ny, nz, scal...  31.8 us
    pallas_call x1, Pallas kernels, on_device(): pl.pallas_call(functools.partial(finish, ch, taps), out_shape=(jax.ShapeD...  2.09 us

profile of v5, /device:TPU:0, one launch (start us, length us, event | category | flops | bytes accessed | tf_op | source)
XLA Modules:
  0.0 34.5 jit_solution(10153205478779795368)
XLA Ops:
  0.6 31.8 %shard_map.93 = (bf16[256,256]{1,0:T(8,128)(2,1)}, bf16[256,256]{1,0:T(8,128)(2,1)}, f32[16,512]{1,0:T(8,128)}) custom-call(s32[1,3]{1,0:T(1,128)} %off_ref.1, s32[1,3]{1,0:T(1,128)} %flip_ref.1, bf16[256,256]{1,0:T(8,128)(2,1)} %bitcast.12, bf16[256,27]{1,0:T(8,128)(2,1)} %bitcast.17, f32[1,16]{1,0:T(1,128)} %bitcast.18, bf16[256,256]{1,0:T(8,128)(2,1)} %bitcast.13), custom_call_target="tpu_custom_call" | custom-call | flops 169869312 | bytes 524288 | tf_op jit(solution)/shard_map/pallas_call | solution.py:432
  32.4 2.1 %shard_map.94 = (bf16[256,256]{1,0:T(8,128)(2,1)}, bf16[256,256]{1,0:T(8,128)(2,1)}, f32[256,27]{1,0:T(8,128)}, f32[1,16]{1,0:T(1,128)}) custom-call(bf16[256,256]{1,0:T(8,128)(2,1)} %get-tuple-element.11.hid_in, bf16[256,256]{1,0:T(8,128)(2,1)} %get-tuple-element.12.gin_in, f32[16,512]{1,0:T(8,128)} %get-tuple-element.13.gw_in), custom_call_target="tpu_custom_call" | custom-call | tf_op jit(solution)/shard_map/pallas_call | solution.py:478

commit v6 on v5

--- a/solution.py
+++ b/solution.py
@@ -52,7 +52,8 @@
     n, dps, planes, ch, ny, nz, scale,
     off_ref, flip_ref, feat_ref, weight_ref, bias_ref, cot_ref,
     hid_out, gin_out, gw_out,
-    hid_ref, gin_ref, gw_ref, feat, weight, cot_in, send1, recv1, stag, recv2, cols, gcols, gext, rs, rsr, zr, ag,
+    hid_ref, gin_ref, gw_ref, feat, weight, cot_in, send1, recv1, stag, recv2,
+    zs, gz, wf, wb, shift, cot, hid, gin, gext, rs, rsr, zr, ag,
     load_sems, store_sems, send_sems, recv_sems,
 ):
     me, my_dp = lax.axis_index("gx"), lax.axis_index("dp")
@@ -149,11 +150,13 @@
     bias = jnp.sum(
         jnp.where(iota((ch, 1), 0) == iota((1, ch), 1), bias_ref[...], 0.0), axis=1, keepdims=True
     )
-    z_less = one_hot(zi == ((zo - 1) & (nz - 1)))
-    z_more = one_hot(zi == ((zo + 1) & (nz - 1)))
-    cols[width : width + ch] = jnp.ones((ch, cols.shape[1]), bf16)
+    for k in range(9):
+        wf[k] = w_fwd[:, k * 3 * ch : (k + 1) * 3 * ch]
+        wb[k] = w_bwd[:, k * 3 * ch : (k + 1) * 3 * ch]
+    shift[0] = one_hot(zi == ((zo - 1) & (nz - 1)))
+    shift[1] = one_hot(zi == ((zo + 1) & (nz - 1)))
     loads[2].wait()
-    cot = mm(order, cot_in[...])
+    cot[...] = mm(order, cot_in[...]).reshape(cot.shape)
 
     sources = []
     for p in range(chunks * planes + 2):
@@ -166,7 +169,7 @@
     def routed(p):
         return recv1[sources[p]]
 
-    first, last = planes, planes + 1
+    first, last = planes + 1, planes
     for q in range(chunks):
         for x in range(planes):
             plane = routed(q * planes + x + 1)
@@ -193,58 +196,68 @@
     each_peer(chunks, functools.partial(start2, planes, 2))
     recv2[my_chunk] = stag[my_chunk]
 
-    def lane(x, y):
-        return (x * ny + y) * nz
-
-    def columns(p):
-        slot = first if p == 0 else last if p == planes + 1 else p - 1
-        mid = [
-            jnp.concatenate([recv2[2 * y, slot], recv2[2 * y + 1, slot]], axis=1)
-            for y in range(ny)
+    def build(target, block, slot, less):
+        stacked = jnp.concatenate([block(slot, y) for y in range(ny)], axis=0)
+        shifted = [
+            mm(stacked, shift[less]).astype(bf16),
+            stacked,
+            mm(stacked, shift[1 - less]).astype(bf16),
         ]
-        stacked = jnp.concatenate(mid, axis=0)
-        shifts = [mm(stacked, z_less).astype(bf16), stacked, mm(stacked, z_more).astype(bf16)]
-        for a in range(3):
-            x = p - a
-            if not 0 <= x < planes:
-                continue
-            for e in range(3):
-                for h in range(3):
-                    t = 9 * a + 3 * e + h
-                    for y in range(ny):
-                        s = (y + e - 1) % ny
-                        cols[t * ch : t * ch + ch, lane(x, y) : lane(x, y) + nz] = shifts[h][
-                            s * ch : s * ch + ch
-                        ]
+        for y in range(ny):
+            for h in range(3):
+                target[slot, y, h * ch : h * ch + ch] = shifted[h][y * ch : y * ch + ch]
+
+    def build_forward(slot, _):
+        build(
+            zs,
+            lambda at, y: jnp.concatenate([recv2[2 * y, at], recv2[2 * y + 1, at]], axis=1),
+            slot, 0,
+        )
+        return 0
+
+    def build_backward(slot, _):
+        build(gz, lambda at, y: gext[at, y], slot, 1)
+        return 0
+
+    step = 4
+    per_plane = ny // step
+    pairs = [(a, e) for a in range(3) for e in range(3)]
+
+    def conv_blocks(i, sums):
+        sums = list(sums)
+        x, y0 = i // per_plane, (i % per_plane) * step
+        for j in range(step):
+            y = y0 + j
+            at = [(lax.rem(x + a + planes + 1, planes + 2), (y + e - 1) & (ny - 1)) for a, e in pairs]
+            pre = bias
+            for k in range(9):
+                pre = pre + mm(wf[k], zs[at[k]])
+            act, slope = gelu_parts(pre)
+            hid[x * ny + y] = act.astype(bf16)
+            grad = (cot[x * ny + y] * slope).astype(bf16)
+            gext[x, y] = grad
+            for k in range(9):
+                sums[k] = sums[k] + mm_t(grad, zs[at[k]])
+            sums[9] = sums[9] + grad.astype(f32)
+        return tuple(sums)
+
+    def grad_blocks(i, _):
+        x, y0 = i // per_plane, (i % per_plane) * step
+        for j in range(step):
+            y = y0 + j
+            total = jnp.zeros((ch, nz), f32)
+            for k, (a, e) in enumerate(pairs):
+                slot = lax.rem(x + planes + 3 - a, planes + 2)
+                total = total + mm(wb[k], gz[slot, (y + 1 - e) & (ny - 1)])
+            gin[x * ny + y] = total.astype(bf16)
+        return 0
 
     wait_bytes(recv2.at[pl.ds(0, chunks - 1), pl.ds(0, planes)], recv_sems.at[1])
-    for p in range(1, planes + 1):
-        columns(p)
-
-    part = []
-    for x in range(planes):
-        k0, k1 = max(0, 1 - x) * 9 * ch, min(3, planes + 1 - x) * 9 * ch
-        for y in range(ny):
-            at = slice(lane(x, y), lane(x, y) + nz)
-            part.append(mm(w_fwd[:, k0:k1], cols[k0:k1, at]) + bias)
-
+    lax.fori_loop(0, planes, build_forward, 0)
     wait_bytes(recv2.at[pl.ds(0, chunks - 1), pl.ds(planes, 2)], recv_sems.at[7])
-    columns(0)
-    columns(planes + 1)
-
-    hidden = []
-    for x in range(planes):
-        for y in range(ny):
-            r0 = (x * ny + y) * ch
-            at = slice(lane(x, y), lane(x, y) + nz)
-            pre = part[x * ny + y]
-            if x == 0:
-                pre = pre + mm(w_fwd[:, : 9 * ch], cols[: 9 * ch, at])
-            if x == planes - 1:
-                pre = pre + mm(w_fwd[:, 18 * ch :], cols[18 * ch : width, at])
-            act, slope = gelu_parts(pre)
-            hidden.append(act.astype(bf16))
-            gext[x + 1, y] = (cot[r0 : r0 + ch] * slope).astype(bf16)
+    lax.fori_loop(planes, planes + 2, build_forward, 0)
+    zeros = (jnp.zeros((ch, 3 * ch), f32),) * 9 + (jnp.zeros((ch, nz), f32),)
+    sums = lax.fori_loop(0, planes * per_plane, conv_blocks, zeros)
 
     right, left = lax.rem(me + 1, n), lax.rem(me + n - 1, n)
     halos = [
@@ -257,14 +270,14 @@
             device_id_type=MESH,
         )
         for side, (here, there, peer) in enumerate(
-            [(planes, 0, right), (1, planes + 1, left)]
+            [(planes - 1, planes + 1, right), (0, planes, left)]
         )
     ]
-    gw = jnp.zeros((ch, width + ch), f32)
-    for x in range(planes):
-        for y in range(ny):
-            gw = gw + mm_t(gext[x + 1, y], cols[:, lane(x, y) : lane(x, y) + nz])
-    gw = jnp.concatenate([gw, jnp.zeros((ch, 512 - width - ch), f32)], axis=1)
+    gw = jnp.concatenate(
+        list(sums[:9])
+        + [jnp.sum(sums[9], axis=1, keepdims=True), jnp.zeros((ch, 511 - width), f32)],
+        axis=1,
+    )
     groups = ch // per
     for k in range(layer):
         g, q = k % groups, k // groups
@@ -289,27 +302,10 @@
     b_out, b_in = iota((rows, 1), 0), iota((1, rows), 1)
     b_base = ((b_in & (ch - 1)) * planes + b_in // (ch * ny)) * ny
     back = one_hot(b_out == b_base + ((b_in // ch) & (ny - 1)))
-    hid_ref[...] = mm(back, jnp.concatenate(hidden, axis=0)).astype(bf16)
+    hid_ref[...] = mm(back, hid[...].reshape(rows, nz)).astype(bf16)
     stores[0].start()
 
-    def grad_columns(p):
-        stacked = jnp.concatenate([gext[p, y] for y in range(ny)], axis=0)
-        shifts = [mm(stacked, z_more).astype(bf16), stacked, mm(stacked, z_less).astype(bf16)]
-        for a in range(3):
-            x = p + a - 2
-            if not 0 <= x < planes:
-                continue
-            for e in range(3):
-                for h in range(3):
-                    t = 9 * a + 3 * e + h
-                    for y in range(ny):
-                        s = (y + 1 - e) % ny
-                        gcols[t * ch : t * ch + ch, lane(x, y) : lane(x, y) + nz] = shifts[h][
-                            s * ch : s * ch + ch
-                        ]
-
-    for p in range(1, planes + 1):
-        grad_columns(p)
+    lax.fori_loop(0, planes, build_backward, 0)
 
     wait_bytes(rsr.at[pl.ds(0, layer - 1)], recv_sems.at[4])
     total = rsr[0]
@@ -331,8 +327,7 @@
 
     for halo in halos:
         halo.wait()
-    grad_columns(0)
-    grad_columns(planes + 1)
+    lax.fori_loop(planes, planes + 2, build_backward, 0)
 
     wait_bytes(zr.at[pl.ds(0, heights - 1)], recv_sems.at[5])
     total = zr[0]
@@ -352,12 +347,8 @@
 
     each_peer(layer, start_ag)
 
-    grad_in = [
-        mm(w_bwd, gcols[:, lane(x, y) : lane(x, y) + nz]).astype(bf16)
-        for x in range(planes)
-        for y in range(ny)
-    ]
-    gin_ref[...] = mm(back, jnp.concatenate(grad_in, axis=0)).astype(bf16)
+    lax.fori_loop(0, planes * per_plane, grad_blocks, 0)
+    gin_ref[...] = mm(back, gin[...].reshape(rows, nz)).astype(bf16)
 
     stores[1].start()
     wait_bytes(ag.at[pl.ds(0, layer - 1)], recv_sems.at[6])
@@ -449,8 +440,14 @@
             pltpu.VMEM((n * planes, ch, 128), bf16),
             pltpu.VMEM((chunks, planes + 2, ch, 128), bf16),
             pltpu.VMEM((chunks, planes + 2, ch, 128), bf16),
-            pltpu.VMEM((width + ch, cells), bf16),
-            pltpu.VMEM((width, cells), bf16),
+            pltpu.VMEM((planes + 2, ny, 3 * ch, nz), bf16),
+            pltpu.VMEM((planes + 2, ny, 3 * ch, nz), bf16),
+            pltpu.VMEM((9, ch, 3 * ch), bf16),
+            pltpu.VMEM((9, ch, 3 * ch), bf16),
+            pltpu.VMEM((2, nz, nz), bf16),
+            pltpu.VMEM((planes * ny, ch, nz), f32),
+            pltpu.VMEM((planes * ny, ch, nz), bf16),
+            pltpu.VMEM((planes * ny, ch, nz), bf16),
             pltpu.VMEM((planes + 2, ny, ch, nz), bf16),
             pltpu.VMEM((layer, per, 128), f32),
             pltpu.VMEM((layer, per, 128), f32),

time: 34.7 us -> 37.3 us (1.075)
  Pallas kernels: 33.9 us -> 36.5 us
    pallas_call x1, Pallas kernels: 31.8 us -> 34.4 us  [on_device(): pl.pallas_call(functools.partial(kernel, n, dps, planes, ch, ny, nz, scal...]
where the time goes in v6:
time: 37.3 us; the launch traced here: 37.1 us
  Pallas kernels  36.5 us (98%)
  between operations  0.64 us (2%)
    pallas_call x1, Pallas kernels, on_device(): pl.pallas_call(functools.partial(kernel, n, dps, planes, ch, ny, nz, scal...  34.4 us
    pallas_call x1, Pallas kernels, on_device(): pl.pallas_call(functools.partial(finish, ch, taps), out_shape=(jax.ShapeD...  2.09 us

profile of v6, /device:TPU:0, one launch (start us, length us, event | category | flops | bytes accessed | tf_op | source)
XLA Modules:
  0.0 37.1 jit_solution(16104084334436540033)
XLA Ops:
  0.6 34.4 %shard_map.93 = (bf16[256,256]{1,0:T(8,128)(2,1)}, bf16[256,256]{1,0:T(8,128)(2,1)}, f32[16,512]{1,0:T(8,128)}) custom-call(s32[1,3]{1,0:T(1,128)} %off_ref.1, s32[1,3]{1,0:T(1,128)} %flip_ref.1, bf16[256,256]{1,0:T(8,128)(2,1)} %bitcast.12, bf16[256,27]{1,0:T(8,128)(2,1)} %bitcast.17, f32[1,16]{1,0:T(1,128)} %bitcast.18, bf16[256,256]{1,0:T(8,128)(2,1)} %bitcast.13), custom_call_target="tpu_custom_call" | custom-call | flops 169869312 | bytes 524288 | tf_op jit(solution)/shard_map/pallas_call | solution.py:423
  35.0 2.1 %shard_map.94 = (bf16[256,256]{1,0:T(8,128)(2,1)}, bf16[256,256]{1,0:T(8,128)(2,1)}, f32[256,27]{1,0:T(8,128)}, f32[1,16]{1,0:T(1,128)}) custom-call(bf16[256,256]{1,0:T(8,128)(2,1)} %get-tuple-element.11.hid_in, bf16[256,256]{1,0:T(8,128)(2,1)} %get-tuple-element.12.gin_in, f32[16,512]{1,0:T(8,128)} %get-tuple-element.13.gw_in), custom_call_target="tpu_custom_call" | custom-call | tf_op jit(solution)/shard_map/pallas_call | solution.py:475

commit v7 on v6

--- a/solution.py
+++ b/solution.py
@@ -219,45 +219,49 @@
         build(gz, lambda at, y: gext[at, y], slot, 1)
         return 0
 
-    step = 4
-    per_plane = ny // step
-    pairs = [(a, e) for a in range(3) for e in range(3)]
-
-    def conv_blocks(i, sums):
-        sums = list(sums)
-        x, y0 = i // per_plane, (i % per_plane) * step
-        for j in range(step):
-            y = y0 + j
-            at = [(lax.rem(x + a + planes + 1, planes + 2), (y + e - 1) & (ny - 1)) for a, e in pairs]
-            pre = bias
-            for k in range(9):
-                pre = pre + mm(wf[k], zs[at[k]])
-            act, slope = gelu_parts(pre)
+    def slot_of(q):
+        return q % (planes + 2)
+
+    def spread_taps(weights, source, q, sign, out):
+        taps_a = [a for a in range(3) if 0 <= q + sign * (a - 1) < planes]
+        stack = jnp.concatenate([weights[3 * a + e] for a in taps_a for e in range(3)], axis=0)
+        for y in range(ny):
+            part = mm(stack, source[slot_of(q), y])
+            for k, a in enumerate(taps_a):
+                for e in range(3):
+                    r0 = (3 * k + e) * ch
+                    key = (q + sign * (a - 1), (y + sign * (e - 1)) % ny)
+                    piece = part[r0 : r0 + ch]
+                    out[key] = out[key] + piece if key in out else piece
+
+    own, halo_planes = list(range(planes)), [-1, planes]
+    pre, grad_in, grads = {}, {}, {}
+    wait_bytes(recv2.at[pl.ds(0, chunks - 1), pl.ds(0, planes)], recv_sems.at[1])
+    for q in own:
+        build_forward(q, 0)
+        spread_taps(wf, zs, q, -1, pre)
+    wait_bytes(recv2.at[pl.ds(0, chunks - 1), pl.ds(planes, 2)], recv_sems.at[7])
+    for q in halo_planes:
+        build_forward(slot_of(q), 0)
+        spread_taps(wf, zs, q, -1, pre)
+    grad_sum = jnp.zeros((ch, nz), f32)
+    for x in range(planes):
+        for y in range(ny):
+            act, slope = gelu_parts(pre[x, y] + bias)
             hid[x * ny + y] = act.astype(bf16)
-            grad = (cot[x * ny + y] * slope).astype(bf16)
-            gext[x, y] = grad
-            for k in range(9):
-                sums[k] = sums[k] + mm_t(grad, zs[at[k]])
-            sums[9] = sums[9] + grad.astype(f32)
-        return tuple(sums)
-
-    def grad_blocks(i, _):
-        x, y0 = i // per_plane, (i % per_plane) * step
-        for j in range(step):
-            y = y0 + j
-            total = jnp.zeros((ch, nz), f32)
-            for k, (a, e) in enumerate(pairs):
-                slot = lax.rem(x + planes + 3 - a, planes + 2)
-                total = total + mm(wb[k], gz[slot, (y + 1 - e) & (ny - 1)])
-            gin[x * ny + y] = total.astype(bf16)
-        return 0
-
-    wait_bytes(recv2.at[pl.ds(0, chunks - 1), pl.ds(0, planes)], recv_sems.at[1])
-    lax.fori_loop(0, planes, build_forward, 0)
-    wait_bytes(recv2.at[pl.ds(0, chunks - 1), pl.ds(planes, 2)], recv_sems.at[7])
-    lax.fori_loop(planes, planes + 2, build_forward, 0)
-    zeros = (jnp.zeros((ch, 3 * ch), f32),) * 9 + (jnp.zeros((ch, nz), f32),)
-    sums = lax.fori_loop(0, planes * per_plane, conv_blocks, zeros)
+            grads[x, y] = (cot[x * ny + y] * slope).astype(bf16)
+            gext[x, y] = grads[x, y]
+            grad_sum = grad_sum + grads[x, y].astype(f32)
+    sums = [jnp.zeros((3 * ch, 3 * ch), f32) for _ in range(3)]
+    for q in own + halo_planes:
+        taps_a = [a for a in range(3) if 0 <= q - a + 1 < planes]
+        for y in range(ny):
+            stack = jnp.concatenate(
+                [gext[q - a + 1, (y - e + 1) % ny] for a in taps_a for e in range(3)], axis=0
+            )
+            part = mm_t(stack, zs[slot_of(q), y])
+            for k, a in enumerate(taps_a):
+                sums[a] = sums[a] + part[k * 3 * ch : (k + 1) * 3 * ch]
 
     right, left = lax.rem(me + 1, n), lax.rem(me + n - 1, n)
     halos = [
@@ -274,8 +278,8 @@
         )
     ]
     gw = jnp.concatenate(
-        list(sums[:9])
-        + [jnp.sum(sums[9], axis=1, keepdims=True), jnp.zeros((ch, 511 - width), f32)],
+        [sums[a][e * ch : e * ch + ch] for a in range(3) for e in range(3)]
+        + [jnp.sum(grad_sum, axis=1, keepdims=True), jnp.zeros((ch, 511 - width), f32)],
         axis=1,
     )
     groups = ch // per
@@ -305,7 +309,9 @@
     hid_ref[...] = mm(back, hid[...].reshape(rows, nz)).astype(bf16)
     stores[0].start()
 
-    lax.fori_loop(0, planes, build_backward, 0)
+    for q in own:
+        build_backward(q, 0)
+        spread_taps(wb, gz, q, 1, grad_in)
 
     wait_bytes(rsr.at[pl.ds(0, layer - 1)], recv_sems.at[4])
     total = rsr[0]
@@ -327,7 +333,8 @@
 
     for halo in halos:
         halo.wait()
-    lax.fori_loop(planes, planes + 2, build_backward, 0)
+    for q in halo_planes:
+        build_backward(slot_of(q), 0)
 
     wait_bytes(zr.at[pl.ds(0, heights - 1)], recv_sems.at[5])
     total = zr[0]
@@ -347,7 +354,11 @@
 
     each_peer(layer, start_ag)
 
-    lax.fori_loop(0, planes * per_plane, grad_blocks, 0)
+    for q in halo_planes:
+        spread_taps(wb, gz, q, 1, grad_in)
+    for x in range(planes):
+        for y in range(ny):
+            gin[x * ny + y] = grad_in[x, y].astype(bf16)
     gin_ref[...] = mm(back, gin[...].reshape(rows, nz)).astype(bf16)
 
     stores[1].start()

time: 37.3 us -> 34 us (0.912)
  Pallas kernels: 36.5 us -> 33.2 us
    pallas_call x1, Pallas kernels: 34.4 us -> 31.1 us  [on_device(): pl.pallas_call(functools.partial(kernel, n, dps, planes, ch, ny, nz, scal...]
where the time goes in v7:
time: 34 us; the launch traced here: 33.8 us
  Pallas kernels  33.2 us (98%)
  between operations  0.64 us (2%)
    pallas_call x1, Pallas kernels, on_device(): pl.pallas_call(functools.partial(kernel, n, dps, planes, ch, ny, nz, scal...  31.1 us
    pallas_call x1, Pallas kernels, on_device(): pl.pallas_call(functools.partial(finish, ch, taps), out_shape=(jax.ShapeD...  2.09 us

profile of v7, /device:TPU:0, one launch (start us, length us, event | category | flops | bytes accessed | tf_op | source)
XLA Modules:
  0.0 33.8 jit_solution(14330263390706700721)
XLA Ops:
  0.6 31.1 %shard_map.93 = (bf16[256,256]{1,0:T(8,128)(2,1)}, bf16[256,256]{1,0:T(8,128)(2,1)}, f32[16,512]{1,0:T(8,128)}) custom-call(s32[1,3]{1,0:T(1,128)} %off_ref.1, s32[1,3]{1,0:T(1,128)} %flip_ref.1, bf16[256,256]{1,0:T(8,128)(2,1)} %bitcast.12, bf16[256,27]{1,0:T(8,128)(2,1)} %bitcast.17, f32[1,16]{1,0:T(1,128)} %bitcast.18, bf16[256,256]{1,0:T(8,128)(2,1)} %bitcast.13), custom_call_target="tpu_custom_call" | custom-call | flops 169869312 | bytes 524288 | tf_op jit(solution)/shard_map/pallas_call | solution.py:434
  31.7 2.1 %shard_map.94 = (bf16[256,256]{1,0:T(8,128)(2,1)}, bf16[256,256]{1,0:T(8,128)(2,1)}, f32[256,27]{1,0:T(8,128)}, f32[1,16]{1,0:T(1,128)}) custom-call(bf16[256,256]{1,0:T(8,128)(2,1)} %get-tuple-element.11.hid_in, bf16[256,256]{1,0:T(8,128)(2,1)} %get-tuple-element.12.gin_in, f32[16,512]{1,0:T(8,128)} %get-tuple-element.13.gw_in), custom_call_target="tpu_custom_call" | custom-call | tf_op jit(solution)/shard_map/pallas_call | solution.py:486

commit v8 on v7

--- a/solution.py
+++ b/solution.py
@@ -252,6 +252,23 @@
             grads[x, y] = (cot[x * ny + y] * slope).astype(bf16)
             gext[x, y] = grads[x, y]
             grad_sum = grad_sum + grads[x, y].astype(f32)
+    right, left = lax.rem(me + 1, n), lax.rem(me + n - 1, n)
+    halos = [
+        pltpu.make_async_remote_copy(
+            src_ref=gext.at[here],
+            dst_ref=gext.at[there],
+            send_sem=send_sems.at[2 + side],
+            recv_sem=recv_sems.at[2 + side],
+            device_id={"gx": peer},
+            device_id_type=MESH,
+        )
+        for side, (here, there, peer) in enumerate(
+            [(planes - 1, planes + 1, right), (0, planes, left)]
+        )
+    ]
+    for halo in halos:
+        halo.start()
+
     sums = [jnp.zeros((3 * ch, 3 * ch), f32) for _ in range(3)]
     for q in own + halo_planes:
         taps_a = [a for a in range(3) if 0 <= q - a + 1 < planes]
@@ -262,21 +279,6 @@
             part = mm_t(stack, zs[slot_of(q), y])
             for k, a in enumerate(taps_a):
                 sums[a] = sums[a] + part[k * 3 * ch : (k + 1) * 3 * ch]
-
-    right, left = lax.rem(me + 1, n), lax.rem(me + n - 1, n)
-    halos = [
-        pltpu.make_async_remote_copy(
-            src_ref=gext.at[here],
-            dst_ref=gext.at[there],
-            send_sem=send_sems.at[2 + side],
-            recv_sem=recv_sems.at[2 + side],
-            device_id={"gx": peer},
-            device_id_type=MESH,
-        )
-        for side, (here, there, peer) in enumerate(
-            [(planes - 1, planes + 1, right), (0, planes, left)]
-        )
-    ]
     gw = jnp.concatenate(
         [sums[a][e * ch : e * ch + ch] for a in range(3) for e in range(3)]
         + [jnp.sum(grad_sum, axis=1, keepdims=True), jnp.zeros((ch, 511 - width), f32)],
@@ -300,8 +302,6 @@
 
     each_peer(layer, start_rs)
     rsr[mine] = rs[mine]
-    for halo in halos:
-        halo.start()
 
     b_out, b_in = iota((rows, 1), 0), iota((1, rows), 1)
     b_base = ((b_in & (ch - 1)) * planes + b_in // (ch * ny)) * ny

time: 34 us -> 34 us (level)
  no operation moved by 1% of the time
where the time goes in v8:
time: 34 us; the launch traced here: 33.9 us
  Pallas kernels  33.2 us (98%)
  between operations  0.64 us (2%)
    pallas_call x1, Pallas kernels, on_device(): pl.pallas_call(functools.partial(kernel, n, dps, planes, ch, ny, nz, scal...  31.1 us
    pallas_call x1, Pallas kernels, on_device(): pl.pallas_call(functools.partial(finish, ch, taps), out_shape=(jax.ShapeD...  2.09 us

profile of v8, /device:TPU:0, one launch (start us, length us, event | category | flops | bytes accessed | tf_op | source)
XLA Modules:
  0.0 33.9 jit_solution(16997062776833693273)
XLA Ops:
  0.6 31.1 %shard_map.93 = (bf16[256,256]{1,0:T(8,128)(2,1)}, bf16[256,256]{1,0:T(8,128)(2,1)}, f32[16,512]{1,0:T(8,128)}) custom-call(s32[1,3]{1,0:T(1,128)} %off_ref.1, s32[1,3]{1,0:T(1,128)} %flip_ref.1, bf16[256,256]{1,0:T(8,128)(2,1)} %bitcast.12, bf16[256,27]{1,0:T(8,128)(2,1)} %bitcast.17, f32[1,16]{1,0:T(1,128)} %bitcast.18, bf16[256,256]{1,0:T(8,128)(2,1)} %bitcast.13), custom_call_target="tpu_custom_call" | custom-call | flops 169869312 | bytes 524288 | tf_op jit(solution)/shard_map/pallas_call | solution.py:434
  31.8 2.1 %shard_map.94 = (bf16[256,256]{1,0:T(8,128)(2,1)}, bf16[256,256]{1,0:T(8,128)(2,1)}, f32[256,27]{1,0:T(8,128)}, f32[1,16]{1,0:T(1,128)}) custom-call(bf16[256,256]{1,0:T(8,128)(2,1)} %get-tuple-element.11.hid_in, bf16[256,256]{1,0:T(8,128)(2,1)} %get-tuple-element.12.gin_in, f32[16,512]{1,0:T(8,128)} %get-tuple-element.13.gw_in), custom_call_target="tpu_custom_call" | custom-call | tf_op jit(solution)/shard_map/pallas_call | solution.py:486
